TPU v7x, 32 devices: a whole 2x2x4 slice. The times are simulated.
32 devices in a mesh: dp: 8 (over y, x, core), seq: 4 (over z).
Axes of the slice: x: 2, y: 2, z: 4, core: 2. Of those that a mesh axis runs over, the one named last changes fastest.
Arguments:
- tokens: bfloat16 [16, 4096, 512], P('dp', 'seq'), may hold values from -6 to 6
- item_lengths: int32 [16, 65], P('dp'), may hold values from 64 to 250, as said below
- w_qkv: bfloat16 [512, 1536], replicated, may hold values from -0.25 to 0.25
- w_out: bfloat16 [512, 512], replicated, may hold values from -6 to 6
- w_up: bfloat16 [512, 2048], replicated, may hold values from -0.25 to 0.25
- w_down: bfloat16 [2048, 512], replicated, may hold values from -0.125 to 0.125
- gain_one: float32 [512], replicated, may hold values from 0.1 to 1.9
- gain_two: float32 [512], replicated, may hold values from 0.1 to 1.9
- cotangent: bfloat16 [16, 4096, 512], P('dp', 'seq'), may hold values from -6 to 6
Outputs:
- output: bfloat16 [16, 4096, 512], P('dp', 'seq')
- grad_tokens: bfloat16 [16, 4096, 512], P('dp', 'seq')
- grad_qkv: float32 [512, 1536], replicated
- grad_out: float32 [512, 512], replicated
- grad_up: float32 [512, 2048], replicated
- grad_down: float32 [2048, 512], replicated
- grad_gain_one: float32 [512], replicated
- grad_gain_two: float32 [512], replicated
Inputs may be any that keep to these rules, and one draw needn't show every extreme that they name: `item_lengths`: each row's items are laid end to end from position 0 in slot order; an item that would end past 4096 and all slots after it are left out, and the rest of the row is empty. Every length is 64, 128 or 250, and no item ends at a multiple of 512 below 4096.
All inputs are finite; a program needn't handle non-finite values.
Results may differ from a plain program's by a relative error of at most 0.013.
Values may be sent and summed in bfloat16 or wider, within the bound.
A program may use at most 192 MiB of HBM per device.

v0:
```python
import functools

import jax
import jax.numpy as jnp
from jax import lax
from jax.experimental import pallas as pl
from jax.experimental.pallas import tpu as pltpu
from jax.sharding import PartitionSpec as P

H = 8
E = 64
SEQ_LEN = 4096
LEN_LONG = 250
HALO = 256
TILE = 256
ENTRIES = 8
BLOCK = 256

EPSILON = 1e-05
NEGATIVE = -1e30
SCALE2 = 0.125 * 1.4426950408889634
GELU_A = 0.7978845608028654
GELU_B = 0.044715
MIB = 2**20
F32 = jnp.float32
BF16 = jnp.bfloat16
NT = (((1,), (1,)), ((), ()))
TN = (((0,), (0,)), ((), ()))
MESH = pl.DeviceIdType.MESH
PIPELINED = 3


def layer_norm(values, scaling):
    centered = values - jnp.mean(values, axis=-1, keepdims=True)
    variance = jnp.mean(centered * centered, axis=-1, keepdims=True)
    return centered * lax.rsqrt(variance + EPSILON) * scaling


def normalize(values):
    centered = values - jnp.mean(values, axis=-1, keepdims=True)
    scale = lax.rsqrt(jnp.mean(centered * centered, axis=-1, keepdims=True) + EPSILON)
    return centered * scale, scale


def normalize_back(upstream, normed, scale):
    mean = jnp.mean(upstream, axis=-1, keepdims=True)
    along = jnp.mean(upstream * normed, axis=-1, keepdims=True)
    return scale * (upstream - mean - normed * along)


def max_tiles(local_len):
    count = 1
    while (count // 2) * 314 + (count % 2) * 64 <= local_len + LEN_LONG - 2:
        count += 1
    return count


def fold_rows(values):
    return jnp.sum(values.reshape(values.shape[0] // 8, 8, values.shape[1]), axis=0)


def plan_tiles(lengths, table, row, tiles):
    slots = lengths.shape[1]
    local_len = tiles[1]
    low = lax.axis_index("seq") * local_len
    high = low + local_len
    base = row * (tiles[0] + 1) * ENTRIES

    def step(k, carry):
        begin, count, tile_begin, in_tile, fitted_end = carry
        true_end = begin + lengths[row, k]
        end = jnp.minimum(true_end, SEQ_LEN)
        touches = (end > low) & (begin < high) & (end > begin)
        fresh = touches & ((count == 0) | (end - tile_begin > TILE))
        count = jnp.where(fresh, count + 1, count)
        tile_begin = jnp.where(fresh, begin, tile_begin)
        in_tile = jnp.where(fresh, 0, in_tile + 1)

        @pl.when(touches)
        def _():
            spot = base + (count - 1) * ENTRIES
            table[spot] = tile_begin - low + HALO
            for j in range(4):

                @pl.when(j >= in_tile)
                def _():
                    table[spot + 1 + j] = end - tile_begin

        fitted_end = jnp.where(true_end <= SEQ_LEN, true_end, fitted_end)
        return (end, count, tile_begin, in_tile, fitted_end)

    zero = jnp.int32(0)
    for b in range(tiles[0]):
        table[base + b * ENTRIES] = 0
    _, count, _, _, fitted_end = lax.fori_loop(0, slots, step, (zero, zero, zero, zero, zero))
    table[base + tiles[0] * ENTRIES] = count
    table[base + tiles[0] * ENTRIES + 1] = fitted_end
    return count


def tile_fills(table, spot):
    def segments(positions):
        return sum((positions >= table[spot + 1 + j]).astype(jnp.int32) for j in range(4))

    seg = segments(lax.broadcasted_iota(jnp.int32, (TILE, 128), 0))
    lane = lax.broadcasted_iota(jnp.int32, (TILE, 128), 1) % E
    same = seg == lane
    one_hot = jnp.where(same, 1.0, 0.0)
    across = jnp.where(same, 0.0, NEGATIVE)
    keys = jnp.where(lane < 5, across, jnp.where(lane < 8, 1.0, 0.0))
    return one_hot, keys


def project_kernel(tokens, w_qkv, gain, projected, normed_t):
    normed, _ = normalize(tokens[...].astype(F32))
    low = (normed * gain[...]).astype(BF16)
    normed_t[...] = low.T
    projected[...] = jnp.dot(low, w_qkv[...], preferred_element_type=F32).astype(BF16)


def project(tokens, w_qkv, gain):
    count, width = tokens.shape
    wide = w_qkv.shape[1]
    block = 2 * BLOCK
    return pl.pallas_call(
        project_kernel,
        grid=(count // block,),
        out_shape=(
            jax.ShapeDtypeStruct((count, wide), BF16),
            jax.ShapeDtypeStruct((width, count), BF16),
        ),
        in_specs=[
            pl.BlockSpec((block, width), lambda i: (i, 0)),
            whole_spec(width, wide),
            whole_spec(1, width),
        ],
        out_specs=(
            pl.BlockSpec((block, wide), lambda i: (i, 0)),
            pl.BlockSpec((width, block), lambda i: (0, i)),
        ),
        compiler_params=pltpu.CompilerParams(vmem_limit_bytes=40 * MIB),
        name="project",
    )(tokens, w_qkv, gain)


def attend_forward_kernel(
    tiles, lengths, local, left, right, w_qkv, gain, mixed, packed, fills, table,
    spread, out, hot, stage, stage_fill, sems,
):
    row = pl.program_id(0)
    local_len = local.shape[0]
    count = plan_tiles(lengths, table, row, tiles)
    for side, tokens in enumerate((left, right)):
        normed = layer_norm(tokens[0].astype(F32), gain[...]).astype(BF16)
        made = jnp.dot(normed, w_qkv[...], preferred_element_type=F32).astype(BF16)
        start = side * (HALO + local_len)
        for c in range(12):
            spread[c, start : start + HALO, :] = made[:, c * 128 : (c + 1) * 128].astype(F32)
    for c in range(12):
        spread[c, HALO : HALO + local_len, :] = local[:, c * 128 : (c + 1) * 128].astype(F32)
    low = lax.broadcasted_iota(jnp.int32, (TILE, 128), 1) < E
    place = lax.broadcasted_iota(jnp.int32, (TILE, 128), 1) % E

    def stores(slot, at):
        return (
            pltpu.make_async_copy(stage.at[slot], packed.at[at], sems.at[0, slot]),
            pltpu.make_async_copy(stage_fill.at[slot], fills.at[at], sems.at[1, slot]),
        )

    def one_tile(b, _):
        spot = (row * (tiles[0] + 1) + b) * ENTRIES
        begin = table[spot]
        slot = lax.rem(b, 2)
        at = row * tiles[0] + b

        @pl.when(b >= 2)
        def _():
            for copy in stores(slot, at - 2):
                copy.wait()

        one_hot, key_fill = tile_fills(table, spot)
        hot[...] = one_hot
        stage_fill[slot, 4] = key_fill.astype(BF16)
        for pair in range(4):
            q = spread[pair, pl.ds(begin, TILE), :].astype(BF16)
            k = spread[4 + pair, pl.ds(begin, TILE), :].astype(BF16)
            v = spread[8 + pair, pl.ds(begin, TILE), :].astype(BF16)
            stage[slot, pair] = q
            stage[slot, 4 + pair] = k
            stage[slot, 8 + pair] = v
            fill_q, fill_k = hot[...].astype(BF16), stage_fill[slot, 4]
            zero = jnp.zeros_like(v)
            made, peaks = 0.0, []
            for side in range(2):
                own = low if side == 0 else ~low
                scores = lax.dot_general(
                    jnp.where(own, q, fill_q),
                    jnp.where(own, k, fill_k),
                    NT,
                    preferred_element_type=F32,
                )
                peak = jnp.max(scores, axis=1, keepdims=True)
                weights = jnp.exp2((scores - peak) * SCALE2).astype(BF16)
                both = jnp.concatenate([jnp.where(own, v, zero), jnp.where(own, zero + 1, zero)], axis=1)
                made += jnp.dot(weights, both, preferred_element_type=F32)
                peaks.append(peak)
            total = made[:, 128:]
            out[pair, pl.ds(begin, TILE), :] = made[:, :128] / total
            total = pltpu.roll(total, E, 1)
            log_sum = jnp.where(low, peaks[1], peaks[0]) + jnp.log2(total) * (1.0 / SCALE2)
            first = log_sum.astype(BF16).astype(F32)
            rest = log_sum - first
            second = rest.astype(BF16).astype(F32)
            fill = jnp.where(place == 7, second - rest, hot[...])
            fill = jnp.where(place == 6, -second, fill)
            stage_fill[slot, pair] = jnp.where(place == 5, -first, fill).astype(BF16)
        for copy in stores(slot, at):
            copy.start()
        return 0

    lax.fori_loop(0, count, one_tile, 0)
    for c in range(4):
        mixed[:, c * 128 : (c + 1) * 128] = out[c, HALO : HALO + local_len, :].astype(BF16)

    @pl.when(count >= 2)
    def _():
        for copy in stores(lax.rem(count, 2), row * tiles[0] + count - 2):
            copy.wait()

    for copy in stores(lax.rem(count + 1, 2), row * tiles[0] + count - 1):
        copy.wait()


def attend_forward(lengths, local, left, right, w_qkv, gain):
    rows = lengths.shape[0]
    width = left.shape[2]
    local_len = local.shape[0] // rows
    most = max_tiles(local_len)
    held = local_len + 2 * HALO
    return pl.pallas_call(
        functools.partial(attend_forward_kernel, (most, local_len)),
        grid=(rows,),
        out_shape=(
            jax.ShapeDtypeStruct((rows * local_len, width), BF16),
            jax.ShapeDtypeStruct((rows * most, 12, TILE, 128), BF16),
            jax.ShapeDtypeStruct((rows * most, 5, TILE, 128), BF16),
            jax.ShapeDtypeStruct((rows * (most + 1) * ENTRIES,), jnp.int32),
        ),
        in_specs=[
            smem_spec(),
            pl.BlockSpec((local_len, 3 * width), lambda r: (r, 0)),
            row_spec(HALO, width),
            row_spec(HALO, width),
            whole_spec(width, 3 * width),
            whole_spec(1, width),
        ],
        out_specs=(
            pl.BlockSpec((local_len, width), lambda r: (r, 0)),
            pl.BlockSpec(memory_space=pl.ANY),
            pl.BlockSpec(memory_space=pl.ANY),
            smem_spec(),
        ),
        scratch_shapes=[
            pltpu.VMEM((12, held, 128), F32),
            pltpu.VMEM((4, held, 128), F32),
            pltpu.VMEM((TILE, 128), F32),
            pltpu.VMEM((2, 12, TILE, 128), BF16),
            pltpu.VMEM((2, 5, TILE, 128), BF16),
            pltpu.SemaphoreType.DMA((2, 2)),
        ],
        compiler_params=pltpu.CompilerParams(vmem_limit_bytes=56 * MIB),
        name="attend_forward",
    )(lengths, local, left, right, w_qkv, gain)


def mlp_kernel(
    tiles, table, tokens, mixed, cotangent, w_out, w_up, w_down, gain,
    output, activated, d_hidden, d_resid, d_attn, d_mixed, normed_t, mixed_t, cotangent_t, grad_gain,
):
    step = pl.program_id(0)
    most, local_len = tiles
    block = tokens.shape[0]
    per_row = local_len // block
    row = step // per_row
    begin = lax.axis_index("seq") * local_len + (step % per_row) * block
    positions = begin + lax.broadcasted_iota(jnp.int32, (block, 1), 0)
    valid = positions < table[(row * (most + 1) + most) * ENTRIES + 1]
    attn = jnp.dot(mixed[...], w_out[...], preferred_element_type=F32)
    resid = tokens[...].astype(F32) + jnp.where(valid, attn, 0.0)
    normed, scale = normalize(resid)
    low = (normed * gain[...]).astype(BF16)
    normed_t[...] = low.T
    mixed_t[...] = mixed[...].T
    dy = cotangent[...]
    cotangent_t[...] = dy.T
    piece = 512
    dense, d_normed = resid, 0.0
    for j in range(w_up.shape[1] // piece):
        columns = slice(j * piece, (j + 1) * piece)
        hidden = jnp.dot(low, w_up[:, columns], preferred_element_type=F32)
        square = hidden * hidden
        bent = jnp.tanh(hidden * (GELU_A + (GELU_A * GELU_B) * square))
        half = 0.5 + 0.5 * bent
        act = (hidden * half).astype(BF16)
        slope = half + (0.5 - 0.5 * bent * bent) * hidden * (GELU_A + (3.0 * GELU_A * GELU_B) * square)
        d_act = lax.dot_general(dy, w_down[columns, :], NT, preferred_element_type=F32)
        grad = (d_act * slope).astype(BF16)
        activated[:, columns] = act
        d_hidden[:, columns] = grad
        dense += jnp.dot(act, w_down[columns, :], preferred_element_type=F32)
        d_normed += lax.dot_general(grad, w_up[:, columns], NT, preferred_element_type=F32)
    output[...] = dense.astype(BF16)

    @pl.when(step == 0)
    def _():
        grad_gain[...] = jnp.zeros_like(grad_gain)

    grad_gain[...] += fold_rows(d_normed * normed)
    made = dy.astype(F32) + normalize_back(d_normed * gain[...], normed, scale)
    d_resid[...] = made
    attn_low = jnp.where(valid, made, 0.0).astype(BF16)
    d_attn[...] = attn_low
    d_mixed[...] = lax.dot_general(attn_low, w_out[...], NT, preferred_element_type=F32).astype(BF16)


def mlp(local_len, table, tokens, mixed, cotangent, w_out, w_up, w_down, gain):
    count, width = tokens.shape
    hidden = w_up.shape[1]
    rows_of = lambda w: pl.BlockSpec((BLOCK, w), lambda i: (i, 0))
    turned = pl.BlockSpec((width, BLOCK), lambda i: (0, i))
    shape = jax.ShapeDtypeStruct
    return pl.pallas_call(
        functools.partial(mlp_kernel, (max_tiles(local_len), local_len)),
        grid=(count // BLOCK,),
        out_shape=(
            shape((count, width), BF16),
            shape((count, hidden), BF16),
            shape((count, hidden), BF16),
            shape((count, width), F32),
            shape((count, width), BF16),
            shape((count, width), BF16),
            shape((width, count), BF16),
            shape((width, count), BF16),
            shape((width, count), BF16),
            shape((8, width), F32),
        ),
        in_specs=[
            smem_spec(),
            rows_of(width),
            rows_of(width),
            rows_of(width),
            whole_spec(width, width),
            whole_spec(width, hidden),
            whole_spec(hidden, width),
            whole_spec(1, width),
        ],
        out_specs=(
            rows_of(width),
            rows_of(hidden),
            rows_of(hidden),
            rows_of(width),
            rows_of(width),
            rows_of(width),
            turned,
            turned,
            turned,
            whole_spec(8, width),
        ),
        compiler_params=pltpu.CompilerParams(vmem_limit_bytes=56 * MIB),
        name="mlp",
    )(table, tokens, mixed, cotangent, w_out, w_up, w_down, gain)


def tile_backward(packed, fills, grad_of, put):
    low = lax.broadcasted_iota(jnp.int32, (TILE, 128), 1) < E
    for pair in range(4):
        q, k, v, o = packed(pair), packed(4 + pair), packed(8 + pair), grad_of(pair)
        fill_q, fill_k = fills(pair), fills(4)
        zero = jnp.zeros_like(q)
        dq, dk, dv = 0.0, 0.0, 0.0
        for side in range(2):
            own = low if side == 0 else ~low
            own_o = jnp.where(own, o, zero)
            scores = lax.dot_general(
                jnp.where(own, k, fill_k), jnp.where(own, q, fill_q), NT, preferred_element_type=F32
            )
            probs = jnp.exp2(scores * SCALE2)
            d_probs = lax.dot_general(v, own_o, NT, preferred_element_type=F32)
            weighted = probs * d_probs
            inner = jnp.sum(weighted, axis=0, keepdims=True)
            d_scores = (weighted - probs * inner).astype(BF16)
            dq += lax.dot_general(d_scores, jnp.where(own, k, zero), TN, preferred_element_type=F32)
            dk += jnp.dot(d_scores, jnp.where(own, q, zero), preferred_element_type=F32)
            dv += jnp.dot(probs.astype(BF16), own_o, preferred_element_type=F32)
        put(pair, (dq * 0.125).astype(BF16))
        put(4 + pair, (dk * 0.125).astype(BF16))
        put(8 + pair, dv.astype(BF16))


def attend_backward_kernel(tiles, table, packed, fills, grad, left, right, made, d_out):
    row, b = pl.program_id(0), pl.program_id(1)
    local_len = tiles[1]

    @pl.when(b == 0)
    def _():
        for c in range(4):
            columns = slice(c * 128, (c + 1) * 128)
            d_out[c, :HALO, :] = left[0, :, columns].astype(F32)
            d_out[c, HALO : HALO + local_len, :] = grad[:, columns].astype(F32)
            d_out[c, HALO + local_len :, :] = right[0, :, columns].astype(F32)

    begin = table[(row * (tiles[0] + 1) + b) * ENTRIES]
    count = table[(row * (tiles[0] + 1) + tiles[0]) * ENTRIES]

    @pl.when(b < count)
    def _():
        def put(c, values):
            made[0, c] = values

        tile_backward(
            lambda c: packed[0, c],
            lambda c: fills[0, c],
            lambda c: d_out[c, pl.ds(begin, TILE), :].astype(BF16),
            put,
        )


def attend_backward(rows, table, packed, fills, grad, left, right):
    local_len, width = grad.shape[0] // rows, grad.shape[1]
    most = max_tiles(local_len)
    held = local_len + 2 * HALO
    tile = lambda n: pl.BlockSpec((1, n, TILE, 128), lambda r, b: (r * most + b, 0, 0, 0))
    halo = pl.BlockSpec((1, HALO, width), lambda r, b: (r, 0, 0))
    return pl.pallas_call(
        functools.partial(attend_backward_kernel, (most, local_len)),
        grid=(rows, most),
        out_shape=jax.ShapeDtypeStruct(packed.shape, BF16),
        in_specs=[
            smem_spec(),
            tile(12),
            tile(5),
            pl.BlockSpec((local_len, width), lambda r, b: (r, 0)),
            halo,
            halo,
        ],
        out_specs=tile(12),
        scratch_shapes=[pltpu.VMEM((4, held, 128), F32)],
        compiler_params=pltpu.CompilerParams(vmem_limit_bytes=56 * MIB),
        name="attend_backward",
    )(table, packed, fills, grad, left, right)


def input_back_kernel(
    tiles, table, tokens, made, d_resid, normed_t, w_qkv, gain, grad_tokens, grad_qkv, grad_gain, spread, total
):
    row = pl.program_id(0)
    most, local_len = tiles
    count = table[(row * (most + 1) + most) * ENTRIES]

    def place(b, _):
        begin = table[(row * (most + 1) + b) * ENTRIES]
        for c in range(12):
            spread[c, pl.ds(begin, TILE), :] = made[b, c].astype(F32)
        return 0

    lax.fori_loop(0, count, place, 0)
    piece = BLOCK
    gain_sum = jnp.zeros(grad_gain.shape, F32)
    for i in range(local_len // piece):
        at = slice(i * piece, (i + 1) * piece)
        d_projected = jnp.concatenate(
            [spread[c, HALO + i * piece : HALO + (i + 1) * piece, :].astype(BF16) for c in range(12)], axis=1
        )
        d_normed = lax.dot_general(d_projected, w_qkv[...], NT, preferred_element_type=F32)
        normed, scale = normalize(tokens[at, :].astype(F32))
        gain_sum += fold_rows(d_normed * normed)
        back = normalize_back(d_normed * gain[...], normed, scale)
        grad_tokens[at, :] = (d_resid[at, :] + back).astype(BF16)

    @pl.when(row == 0)
    def _():
        grad_gain[...] = gain_sum

    @pl.when(row > 0)
    def _():
        grad_gain[...] += gain_sum

    last = row == pl.num_programs(0) - 1
    for c in range(6):
        both = jnp.concatenate(
            [spread[2 * c + i, HALO : HALO + local_len, :].astype(BF16) for i in range(2)], axis=1
        )
        part = jnp.dot(normed_t[...], both, preferred_element_type=F32)
        columns = slice(c * 256, (c + 1) * 256)

        @pl.when(row == 0)
        def _():
            total[:, columns] = part

        @pl.when(row > 0)
        def _():
            total[:, columns] += part

    @pl.when(last)
    def _():
        grad_qkv[...] = total[...].astype(BF16)


def input_back(rows, table, tokens, made, d_resid, normed_t, w_qkv, gain):
    local_len, width = tokens.shape[0] // rows, tokens.shape[1]
    most = max_tiles(local_len)
    held = local_len + 2 * HALO
    wide = w_qkv.shape[1]
    row_block = pl.BlockSpec((local_len, width), lambda r: (r, 0))
    return pl.pallas_call(
        functools.partial(input_back_kernel, (most, local_len)),
        grid=(rows,),
        out_shape=(
            jax.ShapeDtypeStruct(tokens.shape, BF16),
            jax.ShapeDtypeStruct((width, wide), BF16),
            jax.ShapeDtypeStruct((8, width), F32),
        ),
        in_specs=[
            smem_spec(),
            row_block,
            pl.BlockSpec((most, 12, TILE, 128), lambda r: (r, 0, 0, 0)),
            row_block,
            pl.BlockSpec((width, local_len), lambda r: (0, r)),
            whole_spec(width, wide),
            whole_spec(1, width),
        ],
        out_specs=(row_block, whole_spec(width, wide), whole_spec(8, width)),
        scratch_shapes=[pltpu.VMEM((12, held, 128), F32), pltpu.VMEM((width, wide), F32)],
        compiler_params=pltpu.CompilerParams(vmem_limit_bytes=60 * MIB),
        name="input_back",
    )(table, tokens, made, d_resid, normed_t, w_qkv, gain)


def row_spec(*shape):
    return pl.BlockSpec((1,) + shape, lambda r: (r,) + (0,) * len(shape))


def whole_spec(*shape):
    return pl.BlockSpec(shape, lambda r: (0,) * len(shape))


def smem_spec():
    return pl.BlockSpec(memory_space=pltpu.SMEM)


def exchange(values, devices):
    before = lax.ppermute(values[:, -HALO:], "seq", [(i, i + 1) for i in range(devices - 1)])
    after = lax.ppermute(values[:, :HALO], "seq", [(i + 1, i) for i in range(devices - 1)])
    return before, after


def sum_plan(devices):
    dp, seq = devices
    chip = [("dp", 1 << b) for b in range(1, dp.bit_length() - 1)]
    core = [("dp", 1)]
    along = [("seq", 1 << b) for b in range(seq.bit_length() - 1)]
    return [core + chip + along, core + chip[::-1] + along]


def sum_kernel(devices, grads, gains, outs, gains_out, work, slots, done, gain_slots, sems):
    load_sem, store_sem, send_sem, recv_sem, gain_send, gain_recv = sems
    plans = sum_plan(devices)
    steps = len(plans[0])
    chunks = 2 * PIPELINED
    size = work.shape[0] // chunks
    here = {"dp": lax.axis_index("dp"), "seq": lax.axis_index("seq")}

    def other(axis, bit):
        mine = (here[axis] // bit) % 2
        return mine, {axis: here[axis] + bit - 2 * bit * mine}

    barrier = pltpu.get_barrier_semaphore()
    for axis, bit in plans[0]:
        pl.semaphore_signal(barrier, inc=1, device_id=other(axis, bit)[1], device_id_type=MESH)

    pieces = []
    for k, ref in enumerate(grads):
        for c in range(ref.shape[1] // 128):
            pieces.append((k, c, ref.shape[0]))
    loads, stores, at = [[] for _ in range(chunks)], [[] for _ in range(chunks)], 0
    for k, c, rows in pieces:
        inside, summed = work.at[at : at + rows], done.at[at : at + rows]
        chunk = at // size
        loads[chunk].append(
            pltpu.make_async_copy(grads[k].at[:, c * 128 : (c + 1) * 128], inside, load_sem.at[len(loads[chunk]), chunk])
        )
        stores[chunk].append(
            pltpu.make_async_copy(summed, outs[k].at[:, c * 128 : (c + 1) * 128], store_sem.at[len(stores[chunk]), chunk])
        )
        at += rows
    for chunk in range(chunks):
        for copy in loads[chunk]:
            copy.start()
    pl.semaphore_wait(barrier, steps)

    def place(offset, rows):
        return pl.ds(pl.multiple_of(offset, rows), rows)

    def add(offset, slot, rows, into):
        block = min(rows, 256)

        @pl.loop(0, rows // block)
        def _(i):
            mine = work[pl.ds(pl.multiple_of(offset + i * block, block), block), :].astype(F32)
            theirs = slots[pl.ds(pl.multiple_of(slot + i * block, block), block), :].astype(F32)
            into[pl.ds(pl.multiple_of(offset + i * block, block), block), :] = (mine + theirs).astype(BF16)

    def chunk_events(chunk):
        plan = plans[chunk % 2]
        state = {"offset": chunk * size, "rows": size, "slot": chunk * size, "path": []}

        def halve_start(s):
            mine, target = other(*plan[s])
            half = state["rows"] // 2
            keep = state["offset"] + mine * half
            give = state["offset"] + (1 - mine) * half
            copy = pltpu.make_async_remote_copy(
                src_ref=work.at[place(give, half)],
                dst_ref=slots.at[place(state["slot"], half)],
                send_sem=send_sem.at[chunk, s],
                recv_sem=recv_sem.at[chunk, s],
                device_id=target,
                device_id_type=MESH,
            )
            copy.start()
            state["path"].append((keep, give, half))
            state["copy"] = copy

        def halve_end(s):
            keep, _, half = state["path"][s]
            state["copy"].wait()
            add(keep, state["slot"], half, done if s + 1 == steps else work)
            state.update(offset=keep, rows=half, slot=state["slot"] + half)

        def double_start(s):
            _, target = other(*plan[s])
            keep, give, half = state["path"][s]

            def copy_of(offset):
                return pltpu.make_async_remote_copy(
                    src_ref=done.at[place(offset, half)],
                    dst_ref=done.at[place(offset, half)],
                    send_sem=send_sem.at[chunk, steps + s],
                    recv_sem=recv_sem.at[chunk, steps + s],
                    device_id=target,
                    device_id_type=MESH,
                )

            copy_of(keep).start()
            state["copies"] = (copy_of(keep), copy_of(give))

        def double_end(s):
            state["copies"][0].wait_send()
            state["copies"][1].wait_recv()

        def first():
            for copy in loads[chunk]:
                copy.wait()
            halve_start(0)

        def turn(t):
            if t < steps:
                halve_end(t)
            else:
                double_end(2 * steps - 1 - t)
            if t + 1 < steps:
                halve_start(t + 1)
            elif t + 1 < 2 * steps:
                double_start(2 * steps - 2 - t)
            else:
                for copy in stores[chunk]:
                    copy.start()

        return [first] + [functools.partial(turn, t) for t in range(2 * steps)]

    def gain_events():
        plan = plans[0]
        state = {}

        def start(s):
            copy = pltpu.make_async_remote_copy(
                src_ref=gain_slots.at[2 * s],
                dst_ref=gain_slots.at[2 * s + 1],
                send_sem=gain_send.at[s],
                recv_sem=gain_recv.at[s],
                device_id=other(*plan[s])[1],
                device_id_type=MESH,
            )
            copy.start()
            state["copy"] = copy

        def first():
            gain_slots[0] = gains[...]
            start(0)

        def turn(s):
            state["copy"].wait()
            total = gain_slots[2 * s] + gain_slots[2 * s + 1]
            if s + 1 < steps:
                gain_slots[2 * s + 2] = total
                start(s + 1)
            else:
                gains_out[...] = total

        return [first] + [functools.partial(turn, s) for s in range(steps)]

    runs = [(chunk // 2, chunk_events(chunk)) for chunk in range(chunks)]
    runs.append((0, gain_events()))
    last = max(lag + len(events) for lag, events in runs)
    for t in range(last):
        for lag, events in runs:
            if 0 <= t - lag < len(events):
                events[t - lag]()
    for chunk in range(chunks):
        for copy in stores[chunk]:
            copy.wait()


def sum_grads(devices, grads, gains):
    count = len(grads)
    total_rows = sum(g.shape[0] * g.shape[1] // 128 for g in grads)
    steps = len(sum_plan(devices)[0])
    chunks = 2 * PIPELINED

    def kernel(*refs):
        ins, rest = refs[:count], refs[count:]
        gain_ref, outs, rest = rest[0], rest[1 : 1 + count], rest[1 + count :]
        sum_kernel(devices, ins, gain_ref, outs, *rest[:5], rest[5:])

    any_spec = pl.BlockSpec(memory_space=pl.ANY)
    vmem = pl.BlockSpec(memory_space=pltpu.VMEM)
    made = pl.pallas_call(
        kernel,
        out_shape=[jax.ShapeDtypeStruct(g.shape, BF16) for g in grads]
        + [jax.ShapeDtypeStruct(gains.shape, F32)],
        in_specs=[any_spec] * count + [vmem],
        out_specs=[any_spec] * count + [vmem],
        scratch_shapes=[
            pltpu.VMEM((total_rows, 128), BF16),
            pltpu.VMEM((total_rows, 128), BF16),
            pltpu.VMEM((total_rows, 128), BF16),
            pltpu.VMEM((2 * steps,) + gains.shape, F32),
            pltpu.SemaphoreType.DMA((8, chunks)),
            pltpu.SemaphoreType.DMA((8, chunks)),
            pltpu.SemaphoreType.DMA((chunks, 2 * steps)),
            pltpu.SemaphoreType.DMA((chunks, 2 * steps)),
            pltpu.SemaphoreType.DMA((steps,)),
            pltpu.SemaphoreType.DMA((steps,)),
        ],
        compiler_params=pltpu.CompilerParams(
            collective_id=0, has_side_effects=True, vmem_limit_bytes=40 * MIB
        ),
        name="sum_grads",
    )(*grads, gains)
    return made[:count], made[count]


def body(
    devices, tokens, item_lengths, w_qkv, w_out, w_up, w_down, gain_one, gain_two, cotangent
):
    rows, local_len, width = tokens.shape
    count = rows * local_len
    gain_one, gain_two = gain_one.reshape(1, width), gain_two.reshape(1, width)
    flat = tokens.reshape(count, width)
    left, right = exchange(tokens, devices[1])
    projected, normed_one_t = project(flat, w_qkv, gain_one)
    mixed, packed, fills, table = attend_forward(item_lengths, projected, left, right, w_qkv, gain_one)
    (
        output, activated, d_hidden, d_resid, d_attn, d_mixed, normed_two_t, mixed_t, cotangent_t, grad_gain_two
    ) = mlp(local_len, table, flat, mixed, cotangent.reshape(count, width), w_out, w_up, w_down, gain_two)
    d_left, d_right = exchange(d_mixed.reshape(rows, local_len, width), devices[1])
    grad_down = jnp.dot(cotangent_t, activated, preferred_element_type=F32).astype(BF16).T
    grad_up = jnp.dot(normed_two_t, d_hidden, preferred_element_type=F32).astype(BF16)
    grad_out = jnp.dot(mixed_t, d_attn, preferred_element_type=F32).astype(BF16)
    made = attend_backward(rows, table, packed, fills, d_mixed, d_left, d_right)
    grad_tokens, grad_qkv, grad_gain_one = input_back(
        rows, table, flat, made, d_resid, normed_one_t, w_qkv, gain_one
    )
    gains = jnp.concatenate([grad_gain_one, grad_gain_two])
    summed, gains = sum_grads(devices, [grad_qkv, grad_out, grad_up, grad_down], gains)
    grads = tuple(g.astype(F32) for g in summed)
    gains = jnp.sum(gains.reshape(2, 8, width), axis=1)
    placed = (output.reshape(tokens.shape), grad_tokens.reshape(tokens.shape))
    return placed + grads + (gains[0], gains[1])


def solution(mesh):
    rows = P("dp", "seq", None)
    placed = (rows, P("dp", None), P(), P(), P(), P(), P(), P(), rows)
    return jax.shard_map(
        functools.partial(body, (mesh.shape["dp"], mesh.shape["seq"])),
        mesh=mesh,
        in_specs=placed,
        out_specs=(rows, rows, P(), P(), P(), P(), P(), P()),
        check_vma=False,
    )
```

profile of v0, /device:TPU:0, one launch (start us, length us, event | category | flops | bytes accessed | tf_op | source)
XLA Modules:
  0.0 264.3 jit_solution(1039144884688208775)
XLA Ops:
  0.6 0.0 copy-start
  0.6 0.0 copy-start.6
  0.7 1.4 fusion.1
  2.1 1.3 collective-permute-start.1
  3.4 5.6 %collective-permute-start = (bf16[2,256,512]{2,1,0:T(8,128)(2,1)S(1)}, bf16[2,256,512]{2,1,0:T(8,128)(2,1)S(1)}, u32[]{:S(2)}, u32[]{:S(2)}) collective-permute-start(bf16[2,256,512]{2,1,0:T(8,128)(2,1)S(1)} %get-tuple-element.59), channel_id=1, source_target_pairs={{0,1},{1,2},{2,3},{4,5},{5,6},{6,7},{8,9},{9,10},{10,11},{12,13},{... | collective-permute-start | bytes 1572872 | tf_op jit(solution)/shard_map/ppermute | solution.py:552
  9.0 0.0 copy-done
  9.0 0.0 copy-done.6
  9.0 0.0 copy-start.1
  9.0 1.4 copy-done.1
  10.4 5.2 %project.1 = (bf16[2048,1536]{1,0:T(8,128)(2,1)S(1)}, bf16[512,2048]{1,0:T(8,128)(2,1)S(1)}) custom-call(bf16[2048,512]{1,0:T(8,128)(2,1)S(1)} %bitcast.19, bf16[512,1536]{1,0:T(8,128)(2,1)S(1)} %copy-done.1, f32[1,512]{1,0:T(1,128)S(1)} %bitcast.22), custom_call_target="tpu_custom_call" | custom-call | tf_op jit(solution)/shard_map/project/pallas_call | solution.py:125
  15.6 0.0 copy-start.2
  15.6 2.6 copy-done.2
  18.2 0.0 copy-start.3
  18.2 1.3 copy-done.3
  19.5 0.0 collective-permute-done.1.right
  19.5 0.0 copy-start.9
  19.5 0.6 collective-permute-done.left
  20.1 0.0 copy-start.10
  20.1 0.2 copy-done.9
  20.3 0.6 copy-done.10
  20.9 23.3 %attend_forward.1 = (bf16[2048,512]{1,0:T(8,128)(2,1)}, bf16[18,12,256,128]{3,2,1,0:T(8,128)(2,1)}, bf16[18,5,256,128]{3,2,1,0:T(8,128)(2,1)}, s32[160]{0:T(256)}) custom-call(s32[2,65]{1,0:T(2,128)} %lengths.1, bf16[2048,1536]{1,0:T(8,128)(2,1)} %copy-done.2, bf16[2,256,512]{2,1,0:T(8,128)(2,1)} %copy-done.10, bf16[2,256,512]{2,1,0:T(8,128)(2,1)} %copy-done.9, ...), custom_call_target="tpu_custom_call" | custom-call | tf_op jit(solution)/shard_map/attend_forward/pallas_call | solution.py:240
  44.2 35.3 %mlp.1 = (bf16[2048,512]{1,0:T(8,128)(2,1)}, bf16[2048,2048]{1,0:T(8,128)(2,1)}, bf16[2048,2048]{1,0:T(8,128)(2,1)}, f32[2048,512]{1,0:T(8,128)}, bf16[2048,512]...) custom-call(s32[160]{0:T(256)} %get-tuple-element.33.table, ...), custom_call_target="tpu_custom_call" | custom-call | tf_op jit(solution)/shard_map/mlp/pallas_call | solution.py:332
  79.5 0.0 copy-start.15
  79.5 0.0 slice-start
  79.5 1.4 fusion
  81.0 1.4 collective-permute-start.3
  82.4 9.0 %collective-permute-start.2 = (bf16[2,256,512]{2,1,0:T(8,128)(2,1)S(1)}, bf16[2,256,512]{2,1,0:T(8,128)(2,1)S(1)}, u32[]{:S(2)}, u32[]{:S(2)}) collective-permute-start(bf16[2,256,512]{2,1,0:T(8,128)(2,1)S(1)} %get-tuple-element.57), channel_id=1, source_target_pairs={{0,1},{1,2},{2,3},{4,5},{5,6},{6,7},{8,9},{9,10},{10,11},{12,13},{... | collective-permute-start | bytes 1572872 | tf_op jit(solution)/shard_map/ppermute | solution.py:552
  91.5 0.0 copy-done.15
  91.5 0.0 slice-start.1
  91.5 0.0 copy-start.14
  91.5 8.7 %convolution_convert_fusion.refs_3_ = bf16[2048,512]{1,0:T(8,128)(2,1)S(1)} fusion(bf16[2048,2048]{1,0:T(8,128)(2,1)} %get-tuple-element.47, bf16[512,2048]{1,0:T(8,128)(2,1)S(1)} %copy-done.15), kind=kOutput, calls=%fused_computation | convolution fusion | flops 4296015872 | bytes 12582912 | tf_op jit(solution)/shard_map/dot_general | solution.py:777
  100.2 0.0 slice-done
  100.2 0.0 slice-done.1
  100.2 0.0 copy-done.14
  100.2 0.0 copy-start.12
  100.2 0.0 copy-start.13
  100.2 5.8 %convolution_convert_fusion.1.refs_2_ = bf16[512,2048]{1,0:T(8,128)(2,1)} fusion(bf16[512,2048]{1,0:T(8,128)(2,1)S(1)} %copy-done.14, bf16[2048,2048]{1,0:T(8,128)(2,1)S(1)} %bitcast.29), kind=kOutput, calls=%fused_computation.1 | convolution fusion | flops 4296015872 | bytes 12582912 | tf_op jit(solution)/shard_map/dot_general | solution.py:778
  106.0 0.0 copy-done.12
  106.0 0.0 copy-done.13
  106.0 1.3 convolution_convert_fusion.2.refs_1_
  107.2 0.0 collective-permute-done.3.right
  107.3 0.0 copy-start.7
  107.3 0.0 collective-permute-done.2.left
  107.3 0.0 copy-start.8
  107.3 0.8 copy-done.7
  108.1 0.2 copy-done.8
  108.2 36.5 %attend_backward.1.made = bf16[18,12,256,128]{3,2,1,0:T(8,128)(2,1)} custom-call(s32[160]{0:T(256)} %get-tuple-element.33.table, bf16[18,12,256,128]{3,2,1,0:T(8,128)(2,1)} %get-tuple-element.36.packed, bf16[18,5,256,128]{3,2,1,0:T(8,128)(2,1)} %get-tuple-element.37.fills, bf16[2048,512]{1,0:T(8,128)(2,1)} %get-tuple-element.38.grad, ...), custom_call_target="tpu_custom_call" | custom-call | tf_op jit(solution)/shard_map/attend_backward/pallas_call | solution.py:434
  144.7 0.0 copy-start.11
  144.7 23.3 %input_back.1 = (bf16[2048,512]{1,0:T(8,128)(2,1)}, bf16[512,1536]{1,0:T(8,128)(2,1)}, f32[8,512]{1,0:T(8,128)}) custom-call(s32[160]{0:T(256)} %get-tuple-element.33.table, bf16[2048,512]{1,0:T(8,128)(2,1)} %bitcast.18, bf16[18,12,256,128]{3,2,1,0:T(8,128)(2,1)} %attend_backward.1.made, f32[2048,512]{1,0:T(8,128)} %get-tuple-element.39.d_resid, ...), custom_call_target="tpu_custom_call" | custom-call | tf_op jit(solution)/shard_map/input_back/pallas_call | solution.py:515
  168.0 0.0 copy-done.11
  168.0 0.7 pad_maximum_fusion.refs_4_
  168.7 0.0 copy-start.4
  168.7 1.6 copy-done.4
  170.3 0.0 copy-start.5
  170.3 1.4 copy-done.5
  171.7 83.7 %sum_grads.1 = (bf16[512,1536]{1,0:T(8,128)(2,1)S(1)}, bf16[512,512]{1,0:T(8,128)(2,1)S(1)}, bf16[512,2048]{1,0:T(8,128)(2,1)S(1)}, bf16[2048,512]{1,0:T(8,128)(2,1)S(1)}, f32[16,512]{1,0:T(8,128)S(1)}) custom-call(bf16[512,1536]{1,0:T(8,128)(2,1)S(1)} %copy-done.5, bf16[512,512]{1,0:T(8,128)(2,1)S(1)} %convolution_convert_fusion.2.refs_1_, ...), custom_call_target="tpu_custom_call" | custom-call | tf_op jit(solution)/shard_map/sum_grads/pallas_call | solution.py:737
  255.4 0.6 fusion.2
  256.0 1.1 convert_element_type.26
  257.1 2.1 convert_element_type.25
  259.2 2.5 convert_element_type.27
  261.7 2.6 convert_element_type.28
  (2 shorter events, 0.0 us)
Async XLA Ops:
  0.6 8.3 %copy-start = (bf16[2,1024,512]{2,1,0:T(8,128)(2,1)S(1)}, bf16[2,1024,512]{2,1,0:T(8,128)(2,1)}, u32[]{:S(2)}) copy-start(bf16[2,1024,512]{2,1,0:T(8,128)(2,1)} %param.9) | copy-start | bytes 6291460
  0.6 8.3 %copy-start.6 = (f32[512]{0:T(512)S(1)}, f32[512]{0:T(512)}, u32[]{:S(2)}) copy-start(f32[512]{0:T(512)} %param.15) | copy-start | bytes 6148
  2.1 17.4 %collective-permute-start.1 = (bf16[2,256,512]{2,1,0:T(8,128)(2,1)S(1)}, bf16[2,256,512]{2,1,0:T(8,128)(2,1)S(1)}, u32[]{:S(2)}, u32[]{:S(2)}) collective-permute-start(bf16[2,256,512]{2,1,0:T(8,128)(2,1)S(1)} %get-tuple-element.58), channel_id=1, source_target_pairs={{1,0},{2,1},{3,2},{5,4},{6,5},{7,6},{9,8},{10,9},{11,10},{13,12},{... | collective-permute-start | bytes 1572872 | tf_op jit(solution)/shard_map/ppermute | solution.py:553
  3.4 16.7 %collective-permute-start = (bf16[2,256,512]{2,1,0:T(8,128)(2,1)S(1)}, bf16[2,256,512]{2,1,0:T(8,128)(2,1)S(1)}, u32[]{:S(2)}, u32[]{:S(2)}) collective-permute-start(bf16[2,256,512]{2,1,0:T(8,128)(2,1)S(1)} %get-tuple-element.59), channel_id=1, source_target_pairs={{0,1},{1,2},{2,3},{4,5},{5,6},{6,7},{8,9},{9,10},{10,11},{12,13},{... | collective-permute-start | bytes 1572872 | tf_op jit(solution)/shard_map/ppermute | solution.py:552
  9.0 1.4 copy-start.1
  15.6 2.6 copy-start.2
  18.2 1.3 copy-start.3
  19.5 0.8 copy-start.9
  20.1 0.8 copy-start.10
  79.5 11.9 %copy-start.15 = (bf16[512,2048]{1,0:T(8,128)(2,1)S(1)}, bf16[512,2048]{1,0:T(8,128)(2,1)}, u32[]{:S(2)}) copy-start(bf16[512,2048]{1,0:T(8,128)(2,1)} %get-tuple-element.48) | copy-start | bytes 6291460
  79.5 20.6 %slice-start = ((s8[8388608]{0:T(1024)(128)(4,1)}), s8[4194304]{0:T(1024)(128)(4,1)S(1)}, s32[]{:S(2)}) async-start(s8[8388608]{0:T(1024)(128)(4,1)} %bitcast.28), calls=%async_computation | async-start | bytes 8388608
  81.0 26.3 %collective-permute-start.3 = (bf16[2,256,512]{2,1,0:T(8,128)(2,1)S(1)}, bf16[2,256,512]{2,1,0:T(8,128)(2,1)S(1)}, u32[]{:S(2)}, u32[]{:S(2)}) collective-permute-start(bf16[2,256,512]{2,1,0:T(8,128)(2,1)S(1)} %get-tuple-element.56), channel_id=1, source_target_pairs={{1,0},{2,1},{3,2},{5,4},{6,5},{7,6},{9,8},{10,9},{11,10},{13,12},{... | collective-permute-start | bytes 1572872 | tf_op jit(solution)/shard_map/ppermute | solution.py:553
  82.4 24.9 %collective-permute-start.2 = (bf16[2,256,512]{2,1,0:T(8,128)(2,1)S(1)}, bf16[2,256,512]{2,1,0:T(8,128)(2,1)S(1)}, u32[]{:S(2)}, u32[]{:S(2)}) collective-permute-start(bf16[2,256,512]{2,1,0:T(8,128)(2,1)S(1)} %get-tuple-element.57), channel_id=1, source_target_pairs={{0,1},{1,2},{2,3},{4,5},{5,6},{6,7},{8,9},{9,10},{10,11},{12,13},{... | collective-permute-start | bytes 1572872 | tf_op jit(solution)/shard_map/ppermute | solution.py:552
  91.5 8.7 %slice-start.1 = ((s8[8388608]{0:T(1024)(128)(4,1)}), s8[4194304]{0:T(1024)(128)(4,1)S(1)}, s32[]{:S(2)}) async-start(s8[8388608]{0:T(1024)(128)(4,1)} %bitcast.28), calls=%async_computation.1 | async-start | bytes 8388608
  91.5 8.7 %copy-start.14 = (bf16[512,2048]{1,0:T(8,128)(2,1)S(1)}, bf16[512,2048]{1,0:T(8,128)(2,1)}, u32[]{:S(2)}) copy-start(bf16[512,2048]{1,0:T(8,128)(2,1)} %get-tuple-element.45) | copy-start | bytes 6291460
  100.2 5.8 %copy-start.12 = (bf16[2048,512]{1,0:T(8,128)(2,1)S(1)}, bf16[2048,512]{1,0:T(8,128)(2,1)}, u32[]{:S(2)}) copy-start(bf16[2048,512]{1,0:T(8,128)(2,1)} %get-tuple-element.44) | copy-start | bytes 6291460
  100.2 5.8 %copy-start.13 = (bf16[512,2048]{1,0:T(8,128)(2,1)S(1)}, bf16[512,2048]{1,0:T(8,128)(2,1)}, u32[]{:S(2)}) copy-start(bf16[512,2048]{1,0:T(8,128)(2,1)} %get-tuple-element.43) | copy-start | bytes 6291460
  107.3 0.8 copy-start.7
  107.3 0.9 copy-start.8
  144.7 23.3 %copy-start.11 = (f32[8,512]{1,0:T(8,128)S(1)}, f32[8,512]{1,0:T(8,128)}, u32[]{:S(2)}) copy-start(f32[8,512]{1,0:T(8,128)} %get-tuple-element.50) | copy-start | bytes 49156
  168.7 1.6 copy-start.4
  170.3 1.4 copy-start.5
where the time goes:
time: 267 us; the launch traced here: 264 us
  Pallas kernels  207 us (78%)
  starting transfers between devices  17.4 us (7%)
  matrix products  15.7 us (6%)
  local copies, waits for them, and re-layouts  13.5 us (5%)
  other arithmetic  9.07 us (3%)
    pallas_call x1, Pallas kernels, sum_grads(): pl.pallas_call(kernel, out_shape=[jax.ShapeDtypeStruct(g.shape, BF16) for...  83.7 us
    pallas_call x1, Pallas kernels, attend_backward(): pl.pallas_call(functools.partial(attend_backward_kernel, (most, local_len...  36.5 us
    pallas_call x1, Pallas kernels, mlp(): pl.pallas_call(functools.partial(mlp_kernel, (max_tiles(local_len), local...  35.3 us
    pallas_call x1, Pallas kernels, attend_forward(): pl.pallas_call(functools.partial(attend_forward_kernel, (most, local_len)...  23.3 us
    pallas_call x1, Pallas kernels, input_back(): pl.pallas_call(functools.partial(input_back_kernel, (most, local_len)), g...  23.3 us
    ppermute x2, starting transfers between devices, exchange(): lax.ppermute(values[:, -HALO:], 'seq', [(i, i + 1) for i in range(devices...  14.6 us
    unnamed x36, local copies, waits for them, and re-layouts  10 us
    dot_general x1, matrix products, body(): jnp.dot(cotangent_t, activated, preferred_element_type=F32).astype(BF16)  8.67 us
  transfers between devices with their start and end apart: 4, of which 1 were waited for; matrix products, arithmetic and copies ran while one was open for 6% of the time, Pallas kernels for 2%

commit v1 on v0

v1 whole, which is shorter than its diff:
```python
import functools

import jax
import jax.numpy as jnp
from jax import lax
from jax.experimental import pallas as pl
from jax.experimental.pallas import tpu as pltpu
from jax.sharding import PartitionSpec as P

H = 8
E = 64
SEQ_LEN = 4096
LEN_LONG = 250
HALO = 256
TILE = 256
ENTRIES = 8
BLOCK = 256
PIECE = 512
WINDOW = 64
GROUPS = 2
EVERY = 4

EPSILON = 1e-05
NEGATIVE = -1e30
SCALE2 = 0.125 * 1.4426950408889634
GELU_A = 0.7978845608028654
GELU_B = 0.044715
MIB = 2**20
F32 = jnp.float32
BF16 = jnp.bfloat16
NT = (((1,), (1,)), ((), ()))
TN = (((0,), (0,)), ((), ()))
MESH = pl.DeviceIdType.MESH


def layer_norm(values, scaling):
    centered = values - jnp.mean(values, axis=-1, keepdims=True)
    variance = jnp.mean(centered * centered, axis=-1, keepdims=True)
    return centered * lax.rsqrt(variance + EPSILON) * scaling


def normalize(values):
    centered = values - jnp.mean(values, axis=-1, keepdims=True)
    scale = lax.rsqrt(jnp.mean(centered * centered, axis=-1, keepdims=True) + EPSILON)
    return centered * scale, scale


def normalize_back(upstream, normed, scale):
    mean = jnp.mean(upstream, axis=-1, keepdims=True)
    along = jnp.mean(upstream * normed, axis=-1, keepdims=True)
    return scale * (upstream - mean - normed * along)


def max_tiles(local_len):
    count = 1
    while (count // 2) * 314 + (count % 2) * 64 <= local_len + LEN_LONG - 2:
        count += 1
    return count


def fold_rows(values):
    return jnp.sum(values.reshape(values.shape[0] // 8, 8, values.shape[1]), axis=0)


def plan_tiles(lengths, table, row, tiles):
    slots = lengths.shape[1]
    local_len = tiles[1]
    low = lax.axis_index("seq") * local_len
    high = low + local_len
    base = row * (tiles[0] + 1) * ENTRIES

    def step(k, carry):
        begin, count, tile_begin, in_tile, fitted_end = carry
        true_end = begin + lengths[row, k]
        end = jnp.minimum(true_end, SEQ_LEN)
        touches = (end > low) & (begin < high) & (end > begin)
        fresh = touches & ((count == 0) | (end - tile_begin > TILE))
        count = jnp.where(fresh, count + 1, count)
        tile_begin = jnp.where(fresh, begin, tile_begin)
        in_tile = jnp.where(fresh, 0, in_tile + 1)

        @pl.when(touches)
        def _():
            spot = base + (count - 1) * ENTRIES
            table[spot] = tile_begin - low + HALO
            for j in range(4):

                @pl.when(j >= in_tile)
                def _():
                    table[spot + 1 + j] = end - tile_begin

        fitted_end = jnp.where(true_end <= SEQ_LEN, true_end, fitted_end)
        return (end, count, tile_begin, in_tile, fitted_end)

    zero = jnp.int32(0)
    for b in range(tiles[0]):
        table[base + b * ENTRIES] = 0
    _, count, _, _, fitted_end = lax.fori_loop(0, slots, step, (zero, zero, zero, zero, zero))
    table[base + tiles[0] * ENTRIES] = count
    table[base + tiles[0] * ENTRIES + 1] = fitted_end
    windows = local_len // WINDOW
    unpack_from = tiles[2] * (tiles[0] + 1) * ENTRIES + row * windows * 4

    def window(w, b):
        at = HALO + w * WINDOW

        def end_of(n):
            return table[base + n * ENTRIES] + table[base + n * ENTRIES + 4]

        b = jnp.where(end_of(b) <= at, b + 1, b)
        cut = end_of(b) - at
        table[unpack_from + w * 4] = b * TILE + at - table[base + b * ENTRIES]
        table[unpack_from + w * 4 + 1] = (b + 1) * TILE - cut
        table[unpack_from + w * 4 + 2] = cut
        return b

    lax.fori_loop(0, windows, window, zero)
    return count


def tile_fills(table, spot):
    def segments(positions):
        return sum((positions >= table[spot + 1 + j]).astype(jnp.int32) for j in range(4))

    seg = segments(lax.broadcasted_iota(jnp.int32, (TILE, 128), 0))
    lane = lax.broadcasted_iota(jnp.int32, (TILE, 128), 1) % E
    same = seg == lane
    one_hot = jnp.where(same, 1.0, 0.0)
    across = jnp.where(same, 0.0, NEGATIVE)
    keys = jnp.where(lane < 5, across, jnp.where(lane < 8, 1.0, 0.0))
    return one_hot, keys


def project_kernel(tokens, w_qkv, gain, projected, normed_t):
    normed, _ = normalize(tokens[...].astype(F32))
    low = (normed * gain[...]).astype(BF16)
    normed_t[...] = low.T
    projected[...] = jnp.dot(low, w_qkv[...], preferred_element_type=F32).astype(BF16)


def project(tokens, w_qkv, gain):
    count, width = tokens.shape
    wide = w_qkv.shape[1]
    block = 2 * BLOCK
    return pl.pallas_call(
        project_kernel,
        grid=(count // block,),
        out_shape=(
            jax.ShapeDtypeStruct((count, wide), BF16),
            jax.ShapeDtypeStruct((width, count), BF16),
        ),
        in_specs=[
            pl.BlockSpec((block, width), lambda i: (i, 0)),
            whole_spec(width, wide),
            whole_spec(1, width),
        ],
        out_specs=(
            pl.BlockSpec((block, wide), lambda i: (i, 0)),
            pl.BlockSpec((width, block), lambda i: (0, i)),
        ),
        compiler_params=pltpu.CompilerParams(vmem_limit_bytes=40 * MIB),
        name="project",
    )(tokens, w_qkv, gain)


def attend_forward_kernel(
    tiles, lengths, local, left, right, w_qkv, gain, mixed, packed, table,
    spread, out, hot, stage, sems,
):
    row = pl.program_id(0)
    local_len = local.shape[0]
    count = plan_tiles(lengths, table, row, tiles)
    for side, tokens in enumerate((left, right)):
        normed = layer_norm(tokens[0].astype(F32), gain[...]).astype(BF16)
        made = jnp.dot(normed, w_qkv[...], preferred_element_type=F32).astype(BF16)
        start = side * (HALO + local_len)
        for c in range(12):
            spread[c, start : start + HALO, :] = made[:, c * 128 : (c + 1) * 128].astype(F32)
    for c in range(12):
        spread[c, HALO : HALO + local_len, :] = local[:, c * 128 : (c + 1) * 128].astype(F32)
    low = lax.broadcasted_iota(jnp.int32, (TILE, 128), 1) < E
    place = lax.broadcasted_iota(jnp.int32, (TILE, 128), 1) % E

    def store(slot, at):
        return pltpu.make_async_copy(stage.at[slot], packed.at[at], sems.at[slot])

    def one_tile(b, _):
        spot = (row * (tiles[0] + 1) + b) * ENTRIES
        begin = table[spot]
        slot = lax.rem(b, 2)
        at = row * tiles[0] + b

        @pl.when(b >= 2)
        def _():
            store(slot, at - 2).wait()

        one_hot, key_fill = tile_fills(table, spot)
        hot[...] = one_hot
        for group in range(GROUPS):
            stage[slot, group, 8] = key_fill.astype(BF16)
        for pair in range(4):
            q = spread[pair, pl.ds(begin, TILE), :].astype(BF16)
            k = spread[4 + pair, pl.ds(begin, TILE), :].astype(BF16)
            v = spread[8 + pair, pl.ds(begin, TILE), :].astype(BF16)
            group, i = pair // 2, pair % 2
            stage[slot, group, i] = q
            stage[slot, group, 2 + i] = k
            stage[slot, group, 4 + i] = v
            fill_q, fill_k = hot[...].astype(BF16), stage[slot, group, 8]
            zero = jnp.zeros_like(v)
            made, peaks = 0.0, []
            for side in range(2):
                own = low if side == 0 else ~low
                scores = lax.dot_general(
                    jnp.where(own, q, fill_q),
                    jnp.where(own, k, fill_k),
                    NT,
                    preferred_element_type=F32,
                )
                peak = jnp.max(scores, axis=1, keepdims=True)
                weights = jnp.exp2((scores - peak) * SCALE2).astype(BF16)
                both = jnp.concatenate([jnp.where(own, v, zero), jnp.where(own, zero + 1, zero)], axis=1)
                made += jnp.dot(weights, both, preferred_element_type=F32)
                peaks.append(peak)
            total = made[:, 128:]
            out[pair, pl.ds(begin, TILE), :] = made[:, :128] / total
            total = pltpu.roll(total, E, 1)
            log_sum = jnp.where(low, peaks[1], peaks[0]) + jnp.log2(total) * (1.0 / SCALE2)
            first = log_sum.astype(BF16).astype(F32)
            rest = log_sum - first
            second = rest.astype(BF16).astype(F32)
            fill = jnp.where(place == 7, second - rest, hot[...])
            fill = jnp.where(place == 6, -second, fill)
            stage[slot, group, 6 + i] = jnp.where(place == 5, -first, fill).astype(BF16)
        store(slot, at).start()
        return 0

    lax.fori_loop(0, count, one_tile, 0)
    for c in range(4):
        mixed[:, c * 128 : (c + 1) * 128] = out[c, HALO : HALO + local_len, :].astype(BF16)

    @pl.when(count >= 2)
    def _():
        store(lax.rem(count, 2), row * tiles[0] + count - 2).wait()

    store(lax.rem(count + 1, 2), row * tiles[0] + count - 1).wait()


def attend_forward(lengths, local, left, right, w_qkv, gain):
    rows = lengths.shape[0]
    width = left.shape[2]
    local_len = local.shape[0] // rows
    most = max_tiles(local_len)
    held = local_len + 2 * HALO
    return pl.pallas_call(
        functools.partial(attend_forward_kernel, (most, local_len, rows)),
        grid=(rows,),
        out_shape=(
            jax.ShapeDtypeStruct((rows * local_len, width), BF16),
            jax.ShapeDtypeStruct((rows * most, GROUPS, 9, TILE, 128), BF16),
            jax.ShapeDtypeStruct(
                (rows * (most + 1) * ENTRIES + rows * (local_len // WINDOW) * 4,), jnp.int32
            ),
        ),
        in_specs=[
            smem_spec(),
            pl.BlockSpec((local_len, 3 * width), lambda r: (r, 0)),
            row_spec(HALO, width),
            row_spec(HALO, width),
            whole_spec(width, 3 * width),
            whole_spec(1, width),
        ],
        out_specs=(
            pl.BlockSpec((local_len, width), lambda r: (r, 0)),
            pl.BlockSpec(memory_space=pl.ANY),
            smem_spec(),
        ),
        scratch_shapes=[
            pltpu.VMEM((12, held, 128), F32),
            pltpu.VMEM((4, held, 128), F32),
            pltpu.VMEM((TILE, 128), F32),
            pltpu.VMEM((2, GROUPS, 9, TILE, 128), BF16),
            pltpu.SemaphoreType.DMA((2,)),
        ],
        compiler_params=pltpu.CompilerParams(vmem_limit_bytes=56 * MIB),
        name="attend_forward",
    )(lengths, local, left, right, w_qkv, gain)


def mlp_kernel(
    tiles, table, tokens, mixed, cotangent, w_out, w_up, w_down, gain,
    output, activated, d_hidden, d_resid, d_attn, d_mixed, normed_t, mixed_t, cotangent_t, grad_gain,
):
    step = pl.program_id(0)
    most, local_len = tiles
    block = tokens.shape[0]
    per_row = local_len // block
    row = step // per_row
    begin = lax.axis_index("seq") * local_len + (step % per_row) * block
    positions = begin + lax.broadcasted_iota(jnp.int32, (block, 1), 0)
    valid = positions < table[(row * (most + 1) + most) * ENTRIES + 1]
    attn = jnp.dot(mixed[...], w_out[...], preferred_element_type=F32)
    resid = tokens[...].astype(F32) + jnp.where(valid, attn, 0.0)
    normed, scale = normalize(resid)
    low = (normed * gain[...]).astype(BF16)
    normed_t[...] = low.T
    mixed_t[...] = mixed[...].T
    dy = cotangent[...]
    cotangent_t[...] = dy.T
    piece = 512
    dense, d_normed = resid, 0.0
    for j in range(w_up.shape[1] // piece):
        columns = slice(j * piece, (j + 1) * piece)
        hidden = jnp.dot(low, w_up[:, columns], preferred_element_type=F32)
        square = hidden * hidden
        bent = jnp.tanh(hidden * (GELU_A + (GELU_A * GELU_B) * square))
        half = 0.5 + 0.5 * bent
        act = (hidden * half).astype(BF16)
        slope = half + (0.5 - 0.5 * bent * bent) * hidden * (GELU_A + (3.0 * GELU_A * GELU_B) * square)
        d_act = lax.dot_general(dy, w_down[columns, :], NT, preferred_element_type=F32)
        grad = (d_act * slope).astype(BF16)
        for part in range(piece // 256):
            activated[j * (piece // 256) + part] = act[:, part * 256 : (part + 1) * 256]
            d_hidden[j * (piece // 256) + part] = grad[:, part * 256 : (part + 1) * 256]
        dense += jnp.dot(act, w_down[columns, :], preferred_element_type=F32)
        d_normed += lax.dot_general(grad, w_up[:, columns], NT, preferred_element_type=F32)
    output[...] = dense.astype(BF16)

    @pl.when(step == 0)
    def _():
        grad_gain[...] = jnp.zeros_like(grad_gain)

    grad_gain[...] += fold_rows(d_normed * normed)
    made = dy.astype(F32) + normalize_back(d_normed * gain[...], normed, scale)
    d_resid[...] = made
    attn_low = jnp.where(valid, made, 0.0).astype(BF16)
    for part in range(attn_low.shape[1] // 256):
        d_attn[part] = attn_low[:, part * 256 : (part + 1) * 256]
    d_mixed[...] = lax.dot_general(attn_low, w_out[...], NT, preferred_element_type=F32).astype(BF16)


def mlp(local_len, table, tokens, mixed, cotangent, w_out, w_up, w_down, gain):
    count, width = tokens.shape
    hidden = w_up.shape[1]
    rows_of = lambda w: pl.BlockSpec((BLOCK, w), lambda i: (i, 0))
    blocks_of = lambda w: pl.BlockSpec((w // 256, BLOCK, 256), lambda i: (0, i, 0))
    turned = pl.BlockSpec((width, BLOCK), lambda i: (0, i))
    shape = jax.ShapeDtypeStruct
    return pl.pallas_call(
        functools.partial(mlp_kernel, (max_tiles(local_len), local_len)),
        grid=(count // BLOCK,),
        out_shape=(
            shape((count, width), BF16),
            shape((hidden // 256, count, 256), BF16),
            shape((hidden // 256, count, 256), BF16),
            shape((count, width), F32),
            shape((width // 256, count, 256), BF16),
            shape((count, width), BF16),
            shape((width, count), BF16),
            shape((width, count), BF16),
            shape((width, count), BF16),
            shape((8, width), F32),
        ),
        in_specs=[
            smem_spec(),
            rows_of(width),
            rows_of(width),
            rows_of(width),
            whole_spec(width, width),
            whole_spec(width, hidden),
            whole_spec(hidden, width),
            whole_spec(1, width),
        ],
        out_specs=(
            rows_of(width),
            blocks_of(hidden),
            blocks_of(hidden),
            rows_of(width),
            blocks_of(width),
            rows_of(width),
            turned,
            turned,
            turned,
            whole_spec(8, width),
        ),
        compiler_params=pltpu.CompilerParams(vmem_limit_bytes=56 * MIB),
        name="mlp",
    )(table, tokens, mixed, cotangent, w_out, w_up, w_down, gain)


def tile_backward(pairs, packed, fills, grad_of, put):
    low = lax.broadcasted_iota(jnp.int32, (TILE, 128), 1) < E
    for pair in range(pairs):
        q, k, v, o = packed(pair), packed(pairs + pair), packed(2 * pairs + pair), grad_of(pair)
        fill_q, fill_k = fills(pair), fills(pairs)
        zero = jnp.zeros_like(q)
        dq, dk, dv = 0.0, 0.0, 0.0
        for side in range(2):
            own = low if side == 0 else ~low
            own_o = jnp.where(own, o, zero)
            scores = lax.dot_general(
                jnp.where(own, k, fill_k), jnp.where(own, q, fill_q), NT, preferred_element_type=F32
            )
            probs = jnp.exp2(scores * SCALE2)
            d_probs = lax.dot_general(v, own_o, NT, preferred_element_type=F32)
            weighted = probs * d_probs
            inner = jnp.sum(weighted, axis=0, keepdims=True)
            d_scores = (weighted - probs * inner).astype(BF16)
            dq += lax.dot_general(d_scores, jnp.where(own, k, zero), TN, preferred_element_type=F32)
            dk += jnp.dot(d_scores, jnp.where(own, q, zero), preferred_element_type=F32)
            dv += jnp.dot(probs.astype(BF16), own_o, preferred_element_type=F32)
        put(pair, dq * 0.125)
        put(pairs + pair, dk * 0.125)
        put(2 * pairs + pair, dv)


def row_spec(*shape):
    return pl.BlockSpec((1,) + shape, lambda r: (r,) + (0,) * len(shape))


def whole_spec(*shape):
    return pl.BlockSpec(shape, lambda r: (0,) * len(shape))


def smem_spec():
    return pl.BlockSpec(memory_space=pltpu.SMEM)


def exchange(values, devices):
    before = lax.ppermute(values[:, -HALO:], "seq", [(i, i + 1) for i in range(devices - 1)])
    after = lax.ppermute(values[:, :HALO], "seq", [(i + 1, i) for i in range(devices - 1)])
    return before, after


def sum_plan(devices):
    dp, seq = devices
    chip = [("dp", 1 << b) for b in range(1, dp.bit_length() - 1)]
    core = [("dp", 1)]
    along = [("seq", 1 << b) for b in range(seq.bit_length() - 1)]
    return [core + chip + along, core + chip[::-1] + along]


def chunk_pieces(devices):
    unit = max(1, 16 * devices[0] * devices[1] // PIECE)
    if unit == 1:
        return [4] * 8 + [5, 5, 3, 3]
    return [unit] * (48 // unit)


class GradSum:
    def __init__(self, devices, work, slots, done, send_sem, recv_sem):
        self.plans = sum_plan(devices)
        self.steps = len(self.plans[0])
        self.work, self.slots, self.done = work, slots, done
        self.send_sem, self.recv_sem = send_sem, recv_sem
        self.here = {"dp": lax.axis_index("dp"), "seq": lax.axis_index("seq")}
        self.sizes = chunk_pieces(devices)
        self.paths, self.active = [], []
        base = 0
        for chunk, pieces in enumerate(self.sizes):
            offset, rows, slot, path = base, pieces * PIECE, base, []
            for axis, bit in self.plan(chunk):
                mine, _ = self.other(axis, bit)
                rows //= 2
                keep, give = offset + mine * rows, offset + (1 - mine) * rows
                path.append((keep, give, slot, rows))
                offset, slot = keep, slot + rows
            self.paths.append(path)
            base += pieces * PIECE

    def plan(self, chunk):
        return self.plans[chunk % 2]

    def other(self, axis, bit):
        mine = (self.here[axis] // bit) % 2
        return mine, {axis: self.here[axis] + bit - 2 * bit * mine}

    def copy(self, chunk, t, source, target, to):
        return pltpu.make_async_remote_copy(
            src_ref=source,
            dst_ref=target,
            send_sem=self.send_sem.at[chunk, t],
            recv_sem=self.recv_sem.at[chunk, t],
            device_id=self.other(*to)[1],
            device_id_type=MESH,
        )

    def halving(self, chunk, s):
        _, give, slot, rows = self.paths[chunk][s]
        source = self.work.at[pl.ds(pl.multiple_of(give, 16), rows)]
        return self.copy(chunk, s, source, self.slots.at[slot : slot + rows], self.plan(chunk)[s])

    def doubling(self, chunk, s, received):
        keep, give, _, rows = self.paths[chunk][s]
        part = self.done.at[pl.ds(pl.multiple_of(give if received else keep, 16), rows)]
        return self.copy(chunk, self.steps + s, part, part, self.plan(chunk)[s])

    def add(self, chunk, s):
        keep, _, slot, rows = self.paths[chunk][s]
        into = self.done if s + 1 == self.steps else self.work
        count = next(n for n in range(1, rows) if rows % (16 * n) == 0 and rows // n <= 512)
        block = rows // count

        @pl.loop(0, count)
        def _(i):
            at = pl.ds(pl.multiple_of(keep + i * block, 16), block)
            theirs = self.slots[pl.ds(pl.multiple_of(slot + i * block, 16), block), :]
            into[at, :] = (self.work[at, :].astype(F32) + theirs.astype(F32)).astype(BF16)

    def event(self, chunk, t):
        steps = self.steps
        if 0 < t <= steps:
            self.halving(chunk, t - 1).wait()
            self.add(chunk, t - 1)
        elif t > steps:
            self.doubling(chunk, 2 * steps - t, False).wait_send()
            self.doubling(chunk, 2 * steps - t, True).wait_recv()
        if t < steps:
            self.halving(chunk, t).start()
        elif t < 2 * steps:
            self.doubling(chunk, 2 * steps - 1 - t, False).start()
        return t == 2 * steps

    def begin(self, chunks):
        for chunk in chunks:
            self.event(chunk, 0)
            self.active.append([chunk, 1])

    def advance(self, finish):
        for entry in list(self.active):
            if self.event(*entry):
                finish(entry[0])
                self.active.remove(entry)
            entry[1] += 1


def backward_kernel(
    devices, tiles, table, gains, w_qkv, gain_one,
    normed_two_t, cotangent_t, mixed_t, normed_one_t, d_hidden, activated, d_attn, d_mixed, tokens, d_resid,
    packed,
    grad_tokens, grad_qkv, grad_out, grad_up, grad_down, gains_out,
    work, slots, done, left_a, left_b, right_block, halo, d_mix, tok, resid, made_tok, d_proj, bins, d_out,
    tile_in, gain_slots, gain_one_sum,
    send_sem, recv_sem, gain_send, gain_recv, halo_sem, load_sem, block_sem, tile_sem, store_sem, out_sem,
):
    most, local_len = tiles
    count = tok.shape[0]
    rows = count // local_len
    seq = lax.axis_index("seq")
    sums = GradSum(devices, work, slots, done, send_sem, recv_sem)
    steps = sums.steps

    barrier = pltpu.get_barrier_semaphore()
    after, before = seq < devices[1] - 1, seq > 0
    peers = [sums.other(axis, bit)[1] for axis, bit in sums.plans[0] if axis == "dp"]
    peers += [{"seq": lax.rem(seq + d, devices[1])} for d in range(1, devices[1])]
    for peer in peers:
        pl.semaphore_signal(barrier, inc=1, device_id=peer, device_id_type=MESH)

    load_a = lambda ref, k: pltpu.make_async_copy(ref, left_a, load_sem.at[k])
    load_b = lambda ref, k: pltpu.make_async_copy(ref, left_b, load_sem.at[k])
    load_block = lambda ref, block, slot: pltpu.make_async_copy(
        ref.at[block], right_block.at[slot], block_sem.at[slot]
    )
    load_mix = pltpu.make_async_copy(d_mixed, d_mix, load_sem.at[4])
    load_tok = pltpu.make_async_copy(tokens, tok, load_sem.at[5])
    load_resid = pltpu.make_async_copy(d_resid, resid, load_sem.at[6])
    load_a(normed_two_t, 0).start()
    load_block(d_hidden, 0, 0).start()
    load_block(d_hidden, 1, 1).start()
    load_b(cotangent_t, 1).start()
    load_mix.start()

    pl.semaphore_wait(barrier, len(peers))

    def halo_copy(side, row):
        start = row * local_len + (local_len - HALO if side == 0 else 0)
        return pltpu.make_async_remote_copy(
            src_ref=d_mixed.at[start : start + HALO],
            dst_ref=halo.at[side, row],
            send_sem=halo_sem.at[0, side, row],
            recv_sem=halo_sem.at[1, side, row],
            device_id={"seq": seq + 1 if side == 0 else seq - 1},
            device_id_type=MESH,
        )

    for side, sends, receives in ((0, after, before), (1, before, after)):

        @pl.when(sends)
        def _():
            for row in range(rows):
                halo_copy(side, row).start()

        @pl.when(jnp.logical_not(receives))
        def _():
            for row in range(rows):
                halo[side, row] = jnp.zeros(halo.shape[2:], BF16)

    homes = [(grad_up, 0, c) for c in range(16)]
    homes += [(grad_down, i * PIECE, c) for i in range(4) for c in range(4)]
    homes += [(grad_out, 0, c) for c in range(4)]
    homes += [(grad_qkv, 0, kind * 4 + 2 * g + i) for g in range(GROUPS) for kind in range(3) for i in range(2)]
    stored = []

    def store(piece):
        ref, row, c = homes[piece]
        return pltpu.make_async_copy(
            done.at[piece * PIECE : (piece + 1) * PIECE],
            ref.at[row : row + PIECE, c * 128 : (c + 1) * 128],
            out_sem.at[piece],
        )

    def finish(chunk):
        first = sum(sums.sizes[:chunk])
        for piece in range(first, first + sums.sizes[chunk]):
            store(piece).start()
            stored.append(piece)

    begun = [0]

    def ready(pieces):
        chunks = []
        while begun[0] < len(sums.sizes) and sum(sums.sizes[: begun[0] + 1]) <= pieces:
            chunks.append(begun[0])
            begun[0] += 1
        sums.begin(chunks)

    def put_columns(base, block, product):
        low = product.astype(BF16)
        for i in range(2):
            at = pl.multiple_of((base + 2 * block + i) * PIECE, PIECE)
            work[pl.ds(at, PIECE), :] = low[:, i * 128 : (i + 1) * 128]

    def put_rows(base, block, product):
        low = product.T.astype(BF16)
        for c in range(4):
            at = (base + (block // 2) * 4 + c) * PIECE + (block % 2) * 256
            work[pl.ds(pl.multiple_of(at, 256), 256), :] = low[:, c * 128 : (c + 1) * 128]

    half = d_hidden.shape[0] // 2
    runs = [
        (left_a, d_hidden, 0, half, 0, put_columns),
        (left_a, d_hidden, half, half, 0, put_columns),
        (left_b, activated, 0, half, 16, put_rows),
        (left_b, activated, half, half, 16, put_rows),
        (left_a, d_attn, 0, 2, 32, put_columns),
    ]
    waits = {0: load_a(normed_two_t, 0), 2: load_b(cotangent_t, 1), 4: load_a(mixed_t, 2)}
    at = 0
    for n, (lhs, ref, first, blocks, base, put) in enumerate(runs):
        if n in waits:
            waits[n].wait()

        def one_block(j, _, n=n, lhs=lhs, ref=ref, first=first, blocks=blocks, base=base, put=put, at=at):
            slot, later = lax.rem(at + j, 3), lax.rem(at + j + 2, 3)
            load_block(ref, first + j, slot).wait()

            @pl.when(j + 2 < blocks)
            def _():
                load_block(ref, first + j + 2, later).start()

            if n + 1 < len(runs):

                @pl.when(j + 2 >= blocks)
                def _():
                    load_block(runs[n + 1][1], runs[n + 1][2] + j + 2 - blocks, later).start()

            put(base, first + j, jnp.dot(lhs[...], right_block[slot], preferred_element_type=F32))
            return 0

        lax.fori_loop(0, blocks, one_block, 0)
        at += blocks
        if n == 1:
            load_a(mixed_t, 2).start()
        if n == 3:
            load_b(normed_one_t, 3).start()
            load_tok.start()
            load_resid.start()
        if n > 0:
            sums.advance(finish)
        if n < 4:
            ready(8 * (n + 1))

    per_group = rows * most
    total = GROUPS * per_group
    unpack_from = rows * (most + 1) * ENTRIES
    windows = local_len // WINDOW

    def load_tile(step, slot):
        group, spot = step // per_group, lax.rem(step, per_group)
        return pltpu.make_async_copy(packed.at[spot, group], tile_in.at[slot], tile_sem.at[slot])

    load_tile(0, 0).start()
    load_mix.wait()
    for side, sends, receives in ((0, after, before), (1, before, after)):

        @pl.when(sends)
        def _():
            for row in range(rows):
                halo_copy(side, row).wait_send()

        @pl.when(receives)
        def _():
            for row in range(rows):
                halo_copy(side, row).wait_recv()

    def one_tile(step, _):
        slot = lax.rem(step, 2)
        group, spot = step // per_group, lax.rem(step, per_group)
        row, b = spot // most, lax.rem(spot, most)
        load_tile(step, slot).wait()

        @pl.when(step + 1 < total)
        def _():
            load_tile(step + 1, 1 - slot).start()

        @pl.when(b == 0)
        def _():
            start = pl.multiple_of(row * local_len, local_len)
            for i in range(2):
                columns = pl.ds(pl.multiple_of((2 * group + i) * 128, 128), 128)
                d_out[i, :HALO, :] = halo[0, row, :, columns].astype(F32)
                d_out[i, HALO : HALO + local_len, :] = d_mix[pl.ds(start, local_len), columns].astype(F32)
                d_out[i, HALO + local_len :, :] = halo[1, row, :, columns].astype(F32)

        begin = table[(row * (most + 1) + b) * ENTRIES]

        def put(c, values):
            bins[c, pl.ds(pl.multiple_of(b * TILE, TILE), TILE), :] = values

        tile_backward(
            2,
            lambda c: tile_in[slot, c],
            lambda c: tile_in[slot, 6 + c],
            lambda c: d_out[c, pl.ds(begin, TILE), :].astype(BF16),
            put,
        )

        @pl.when(b == most - 1)
        def _():
            @pl.loop(0, windows)
            def _(w):
                entry = unpack_from + (row * windows + w) * 4
                one, two, cut = table[entry], table[entry + 1], table[entry + 2]
                in_one = lax.broadcasted_iota(jnp.int32, (WINDOW, 128), 0) < cut
                to = pl.multiple_of(row * local_len + w * WINDOW, WINDOW)
                for c in range(6):
                    values = jnp.where(
                        in_one, bins[c, pl.ds(one, WINDOW), :], bins[c, pl.ds(two, WINDOW), :]
                    )
                    d_proj[group * 6 + c, pl.ds(to, WINDOW), :] = values.astype(BF16)

        def qkv_gradient(g):
            for kind in range(3):
                both = jnp.concatenate([d_proj[g * 6 + 2 * kind + i] for i in range(2)], axis=1)
                product = jnp.dot(left_b[...], both, preferred_element_type=F32).astype(BF16)
                for i in range(2):
                    piece = 36 + 6 * g + 2 * kind + i
                    work[piece * PIECE : (piece + 1) * PIECE, :] = product[:, i * 128 : (i + 1) * 128]

        for k in range(total):
            ends_group = (k + 1) % per_group == 0
            moves = k % EVERY == EVERY - 1 and sums.active
            if not (ends_group or moves):
                continue

            @pl.when(step == k)
            def _():
                if moves:
                    sums.advance(finish)
                if ends_group:
                    g = k // per_group
                    if g == 0:
                        load_b(normed_one_t, 3).wait()
                    qkv_gradient(g)
                    ready(42 + 6 * g)

        return 0

    lax.fori_loop(0, total, one_tile, 0)

    load_tok.wait()
    load_resid.wait()
    gain_one_sum[...] = jnp.zeros_like(gain_one_sum)
    blocks = count // BLOCK

    def store_tok(i):
        part = pl.ds(pl.multiple_of(i * BLOCK, BLOCK), BLOCK)
        return pltpu.make_async_copy(made_tok.at[part], grad_tokens.at[part], store_sem.at[i])

    def input_block(i, _):
        part = pl.ds(pl.multiple_of(i * BLOCK, BLOCK), BLOCK)
        order = [6 * (pair // 2) + 2 * kind + pair % 2 for kind in range(3) for pair in range(4)]
        d_projected = jnp.concatenate([d_proj[c, part, :] for c in order], axis=1)
        d_normed = lax.dot_general(d_projected, w_qkv[...], NT, preferred_element_type=F32)
        normed, scale = normalize(tok[part, :].astype(F32))
        gain_one_sum[...] += fold_rows(d_normed * normed)
        back = normalize_back(d_normed * gain_one[...], normed, scale)
        made_tok[part, :] = (resid[part, :] + back).astype(BF16)
        store_tok(i).start()
        for k in range(1, blocks, 2):

            @pl.when(i == k)
            def _():
                sums.advance(finish)

        return 0

    lax.fori_loop(0, blocks, input_block, 0)

    def gain_copy(s):
        return pltpu.make_async_remote_copy(
            src_ref=gain_slots.at[2 * s],
            dst_ref=gain_slots.at[2 * s + 1],
            send_sem=gain_send.at[s],
            recv_sem=gain_recv.at[s],
            device_id=sums.other(*sums.plans[0][s])[1],
            device_id_type=MESH,
        )

    gain_slots[0, :8] = gain_one_sum[...]
    gain_slots[0, 8:] = gains[...]
    gain_copy(0).start()
    for s in range(steps):
        if sums.active:
            sums.advance(finish)
        gain_copy(s).wait()
        joined = gain_slots[2 * s] + gain_slots[2 * s + 1]
        if s + 1 < steps:
            gain_slots[2 * s + 2] = joined
            gain_copy(s + 1).start()
        else:
            gains_out[...] = joined
    while sums.active:
        sums.advance(finish)
    for i in range(blocks):
        store_tok(i).wait()
    for piece in stored:
        store(piece).wait()


def backward(
    devices, rows, table, gains, w_qkv, gain_one, normed_two_t, cotangent_t, mixed_t, normed_one_t,
    d_hidden, activated, d_attn, d_mixed, tokens, d_resid, packed,
):
    count, width = tokens.shape
    local_len = count // rows
    most = max_tiles(local_len)
    held = local_len + 2 * HALO
    hidden, wide = d_hidden.shape[0] * d_hidden.shape[2], w_qkv.shape[1]
    steps = len(sum_plan(devices)[0])
    chunks = len(chunk_pieces(devices))
    shape = jax.ShapeDtypeStruct
    anywhere = pl.BlockSpec(memory_space=pl.ANY)
    vmem = pl.BlockSpec(memory_space=pltpu.VMEM)
    dma = pltpu.SemaphoreType.DMA
    return pl.pallas_call(
        functools.partial(backward_kernel, devices, (most, local_len)),
        out_shape=(
            shape((count, width), BF16),
            shape((width, wide), BF16),
            shape((width, width), BF16),
            shape((width, hidden), BF16),
            shape((hidden, width), BF16),
            shape((16, width), F32),
        ),
        in_specs=[smem_spec(), vmem, vmem, vmem] + [anywhere] * 11,
        out_specs=(anywhere,) * 5 + (vmem,),
        scratch_shapes=[
            pltpu.VMEM((48 * PIECE, 128), BF16),
            pltpu.VMEM((48 * PIECE, 128), BF16),
            pltpu.VMEM((48 * PIECE, 128), BF16),
            pltpu.VMEM((width, count), BF16),
            pltpu.VMEM((width, count), BF16),
            pltpu.VMEM((3, count, 256), BF16),
            pltpu.VMEM((2, rows, HALO, width), BF16),
            pltpu.VMEM((count, width), BF16),
            pltpu.VMEM((count, width), BF16),
            pltpu.VMEM((count, width), F32),
            pltpu.VMEM((count, width), BF16),
            pltpu.VMEM((12, count, 128), BF16),
            pltpu.VMEM((6, most * TILE + WINDOW, 128), F32),
            pltpu.VMEM((2, held, 128), F32),
            pltpu.VMEM((2, 9, TILE, 128), BF16),
            pltpu.VMEM((2 * steps, 16, width), F32),
            pltpu.VMEM((8, width), F32),
            dma((chunks, 2 * steps)),
            dma((chunks, 2 * steps)),
            dma((steps,)),
            dma((steps,)),
            dma((2, 2, rows)),
            dma((7,)),
            dma((3,)),
            dma((2,)),
            dma((count // BLOCK,)),
            dma((48,)),
        ],
        compiler_params=pltpu.CompilerParams(
            collective_id=0, has_side_effects=True, vmem_limit_bytes=60 * MIB
        ),
        name="backward",
    )(
        table, gains, w_qkv, gain_one, normed_two_t, cotangent_t, mixed_t, normed_one_t,
        d_hidden, activated, d_attn, d_mixed, tokens, d_resid, packed,
    )


def body(
    devices, tokens, item_lengths, w_qkv, w_out, w_up, w_down, gain_one, gain_two, cotangent
):
    rows, local_len, width = tokens.shape
    count = rows * local_len
    gain_one, gain_two = gain_one.reshape(1, width), gain_two.reshape(1, width)
    flat = tokens.reshape(count, width)
    left, right = exchange(tokens, devices[1])
    projected, normed_one_t = project(flat, w_qkv, gain_one)
    mixed, packed, table = attend_forward(item_lengths, projected, left, right, w_qkv, gain_one)
    (
        output, activated, d_hidden, d_resid, d_attn, d_mixed, normed_two_t, mixed_t, cotangent_t, grad_gain_two
    ) = mlp(local_len, table, flat, mixed, cotangent.reshape(count, width), w_out, w_up, w_down, gain_two)
    grad_tokens, grad_qkv, grad_out, grad_up, grad_down, gains = backward(
        devices, rows, table, grad_gain_two, w_qkv, gain_one, normed_two_t, cotangent_t, mixed_t, normed_one_t,
        d_hidden, activated, d_attn, d_mixed, flat, d_resid, packed,
    )
    summed = (grad_qkv, grad_out, grad_up, grad_down)
    grads = tuple(g.astype(F32) for g in summed)
    gains = jnp.sum(gains.reshape(2, 8, width), axis=1)
    placed = (output.reshape(tokens.shape), grad_tokens.reshape(tokens.shape))
    return placed + grads + (gains[0], gains[1])


def solution(mesh):
    rows = P("dp", "seq", None)
    placed = (rows, P("dp", None), P(), P(), P(), P(), P(), P(), rows)
    return jax.shard_map(
        functools.partial(body, (mesh.shape["dp"], mesh.shape["seq"])),
        mesh=mesh,
        in_specs=placed,
        out_specs=(rows, rows, P(), P(), P(), P(), P(), P()),
        check_vma=False,
    )
```

time: 267 us -> 221 us (0.83); the launches traced: 264 us -> 221 us
  Pallas kernels: 207 us -> 191 us
  matrix products: 15.7 us -> 0 us
  starting transfers between devices: 17.4 us -> 6.25 us
  local copies, waits for them, and re-layouts: 13.5 us -> 9.52 us
  waiting for transfers between devices: 0.62 us -> 3.36 us
    pallas_call x4 -> x2, Pallas kernels: 167 us -> 150 us  [the longest x1 126 us: backward(): pl.pallas_call(functools.partial(backward_kernel, devices, (most, local_l...]
    dot_general x3 -> x0, matrix products: 15.7 us -> none  [the longest x1 8.67 us: body(): jnp.dot(cotangent_t, activated, preferred_element_type=F32).astype(BF16)]
    ppermute x2 -> x1, starting transfers between devices: 14.6 us -> 4.96 us  [exchange(): lax.ppermute(values[:, -HALO:], 'seq', [(i, i + 1) for i in range(devices...]
    ppermute x2 -> x1, waiting for transfers between devices: 0.01 us -> 3.36 us  [exchange(): lax.ppermute(values[:, :HALO], 'seq', [(i + 1, i) for i in range(devices...]
    unnamed x36 -> x25, local copies, waits for them, and re-layouts: 10 us -> 7.51 us
  transfers between devices with their start and end apart: 4 -> 2, of which waited for: 1 -> 1; matrix products, arithmetic and copies ran while one was open for 6% -> 0% of each run, Pallas kernels for 2% -> 2%
where the time goes in v1:
time: 221 us
  Pallas kernels  191 us (86%)
  other arithmetic  9.9 us (4%)
  local copies, waits for them, and re-layouts  9.52 us (4%)
  starting transfers between devices  6.25 us (3%)
  waiting for transfers between devices  3.36 us (2%)
    pallas_call x1, Pallas kernels, backward(): pl.pallas_call(functools.partial(backward_kernel, devices, (most, local_l...  126 us
    pallas_call x1, Pallas kernels, mlp(): pl.pallas_call(functools.partial(mlp_kernel, (max_tiles(local_len), local...  36.2 us
    pallas_call x1, Pallas kernels, attend_forward(): pl.pallas_call(functools.partial(attend_forward_kernel, (most, local_len,...  24.4 us
    convert_element_type x4, other arithmetic, body(): grads = tuple((g.astype(F32) for g in summed))  9.88 us
    unnamed x25, local copies, waits for them, and re-layouts  7.51 us
    pallas_call x1, Pallas kernels, project(): pl.pallas_call(project_kernel, grid=(count // block,), out_shape=(jax.Sha...  5.21 us
    ppermute x1, starting transfers between devices, exchange(): lax.ppermute(values[:, -HALO:], 'seq', [(i, i + 1) for i in range(devices...  4.96 us
  transfers between devices with their start and end apart: 2, of which 1 were waited for; matrix products, arithmetic and copies ran while one was open for 0% of the time, Pallas kernels for 2%

profile of v1, /device:TPU:0, one launch (start us, length us, event | category | flops | bytes accessed | tf_op | source)
XLA Modules:
  0.0 221.1 jit_solution(17664799623265520653)
XLA Ops:
  0.6 0.0 copy-start
  0.6 0.0 copy-start.4
  0.7 1.4 fusion
  2.1 5.0 %collective-permute-start = (bf16[2,256,512]{2,1,0:T(8,128)(2,1)S(1)}, bf16[2,256,512]{2,1,0:T(8,128)(2,1)S(1)}, u32[]{:S(2)}, u32[]{:S(2)}) collective-permute-start(bf16[2,256,512]{2,1,0:T(8,128)(2,1)S(1)} %get-tuple-element.51), channel_id=1, source_target_pairs={{0,1},{1,2},{2,3},{4,5},{5,6},{6,7},{8,9},{9,10},{10,11},{12,13},{... | collective-permute-start | bytes 1572872 | tf_op jit(solution)/shard_map/ppermute | solution.py:430
  7.0 1.3 collective-permute-start.1
  8.3 0.0 copy-done
  8.4 0.0 copy-done.4
  8.4 0.0 copy-start.1
  8.4 1.4 copy-done.1
  9.8 5.2 %project.1 = (bf16[2048,1536]{1,0:T(8,128)(2,1)S(1)}, bf16[512,2048]{1,0:T(8,128)(2,1)S(1)}) custom-call(bf16[2048,512]{1,0:T(8,128)(2,1)S(1)} %bitcast.12, bf16[512,1536]{1,0:T(8,128)(2,1)S(1)} %copy-done.1, f32[1,512]{1,0:T(1,128)S(1)} %bitcast.15), custom_call_target="tpu_custom_call" | custom-call | tf_op jit(solution)/shard_map/project/pallas_call | solution.py:145
  15.0 0.0 copy-start.2
  15.0 2.7 %copy-done.2 = bf16[2048,1536]{1,0:T(8,128)(2,1)} copy-done((bf16[2048,1536]{1,0:T(8,128)(2,1)}, bf16[2048,1536]{1,0:T(8,128)(2,1)S(1)}, u32[]{:S(2)}) %copy-start.2) | copy-done | bytes 6291480
  17.7 0.0 copy-start.3
  17.7 1.3 copy-done.3
  19.0 0.0 collective-permute-done.left
  19.0 0.0 copy-start.9
  19.0 3.4 %collective-permute-done.1.right = bf16[2,256,512]{2,1,0:T(8,128)(2,1)S(1)} collective-permute-done((bf16[2,256,512]{2,1,0:T(8,128)(2,1)S(1)}, bf16[2,256,512]{2,1,0:T(8,128)(2,1)S(1)}, u32[]{:S(2)}, u32[]{:S(2)}) %collective-permute-start.1) | collective-permute-done | bytes 524320 | tf_op jit(solution)/shard_map/ppermute | solution.py:431
  22.3 0.0 copy-start.10
  22.3 0.0 copy-done.9
  22.3 0.8 copy-done.10
  23.1 24.4 %attend_forward.1 = (bf16[2048,512]{1,0:T(8,128)(2,1)}, bf16[18,2,9,256,128]{4,3,2,1,0:T(8,128)(2,1)}, s32[288]{0:T(512)}) custom-call(s32[2,65]{1,0:T(2,128)} %lengths.1, bf16[2048,1536]{1,0:T(8,128)(2,1)} %copy-done.2, bf16[2,256,512]{2,1,0:T(8,128)(2,1)} %copy-done.9, bf16[2,256,512]{2,1,0:T(8,128)(2,1)} %copy-done.10, bf16[512,1536]{1,0:T(8,128)(2,1)} %w_qkv.5, ...), custom_call_target="tpu_custom_call" | custom-call | tf_op jit(solution)/shard_map/attend_forward/pallas_call | solution.py:255
  47.5 36.2 %mlp.1 = (bf16[2048,512]{1,0:T(8,128)(2,1)}, bf16[8,2048,256]{2,1,0:T(8,128)(2,1)}, bf16[8,2048,256]{2,1,0:T(8,128)(2,1)}, f32[2048,512]{1,0:T(8,128)}, bf16[2,2...) custom-call(s32[288]{0:T(512)} %get-tuple-element.30.table, ...), custom_call_target="tpu_custom_call" | custom-call | tf_op jit(solution)/shard_map/mlp/pallas_call | solution.py:349
  83.7 125.5 %backward.1 = (bf16[2048,512]{1,0:T(8,128)(2,1)}, bf16[512,1536]{1,0:T(8,128)(2,1)}, bf16[512,512]{1,0:T(8,128)(2,1)}, bf16[512,2048]{1,0:T(8,128)(2,1)}, bf16[2048,512]{1,0:T(8,128)(2,1)}, /*index=5*/f32[16,512]{1,0:T(8,128)}) custom-call(s32[288]{0:T(512)} %get-tuple-element.30.table, f32[8,512]{1,0:T(8,128)} %get-tuple-element.33.gains, ...), custom_call_target="tpu_custom_call" | custom-call | tf_op jit(solution)/shard_map/backward/pallas_call | solution.py:857
  209.2 0.0 copy-start.8
  209.2 0.0 copy-start.6
  209.2 3.6 %convert_element_type.12 = f32[512,1536]{1,0:T(8,128)} convert(bf16[512,1536]{1,0:T(8,128)(2,1)} %get-tuple-element.45) | non-fusion elementwise | flops 786432 | bytes 4718592 | tf_op jit(solution)/shard_map/convert_element_type | solution.py:926
  212.9 0.0 copy-done.8
  212.9 1.1 convert_element_type.13
  214.0 0.0 copy-done.6
  214.0 0.0 copy-start.5
  214.0 2.5 %convert_element_type.14 = f32[512,2048]{1,0:T(8,128)} convert(bf16[512,2048]{1,0:T(8,128)(2,1)S(1)} %copy-done.6) | non-fusion elementwise | flops 1048576 | bytes 6291456 | tf_op jit(solution)/shard_map/convert_element_type | solution.py:926
  216.5 0.0 copy-done.5
  216.5 0.0 copy-start.11
  216.5 0.0 copy-start.7
  216.5 2.6 %convert_element_type.15 = f32[2048,512]{1,0:T(8,128)} convert(bf16[2048,512]{1,0:T(8,128)(2,1)S(1)} %copy-done.5) | non-fusion elementwise | flops 1048576 | bytes 6291456 | tf_op jit(solution)/shard_map/convert_element_type | solution.py:926
  219.1 0.0 copy-done.11
  219.1 0.6 fusion.1
  219.7 0.0 copy-done.7
  219.7 1.3 copy.18
  (1 shorter events, 0.0 us)
Async XLA Ops:
  0.6 7.7 %copy-start = (bf16[2,1024,512]{2,1,0:T(8,128)(2,1)S(1)}, bf16[2,1024,512]{2,1,0:T(8,128)(2,1)}, u32[]{:S(2)}) copy-start(bf16[2,1024,512]{2,1,0:T(8,128)(2,1)} %param.9) | copy-start | bytes 6291460
  0.6 7.7 %copy-start.4 = (f32[512]{0:T(512)S(1)}, f32[512]{0:T(512)}, u32[]{:S(2)}) copy-start(f32[512]{0:T(512)} %param.15) | copy-start | bytes 6148
  2.1 16.9 %collective-permute-start = (bf16[2,256,512]{2,1,0:T(8,128)(2,1)S(1)}, bf16[2,256,512]{2,1,0:T(8,128)(2,1)S(1)}, u32[]{:S(2)}, u32[]{:S(2)}) collective-permute-start(bf16[2,256,512]{2,1,0:T(8,128)(2,1)S(1)} %get-tuple-element.51), channel_id=1, source_target_pairs={{0,1},{1,2},{2,3},{4,5},{5,6},{6,7},{8,9},{9,10},{10,11},{12,13},{... | collective-permute-start | bytes 1572872 | tf_op jit(solution)/shard_map/ppermute | solution.py:430
  7.0 15.3 %collective-permute-start.1 = (bf16[2,256,512]{2,1,0:T(8,128)(2,1)S(1)}, bf16[2,256,512]{2,1,0:T(8,128)(2,1)S(1)}, u32[]{:S(2)}, u32[]{:S(2)}) collective-permute-start(bf16[2,256,512]{2,1,0:T(8,128)(2,1)S(1)} %get-tuple-element.50), channel_id=1, source_target_pairs={{1,0},{2,1},{3,2},{5,4},{6,5},{7,6},{9,8},{10,9},{11,10},{13,12},{... | collective-permute-start | bytes 1572872 | tf_op jit(solution)/shard_map/ppermute | solution.py:431
  8.4 1.4 copy-start.1
  15.0 2.7 %copy-start.2 = (bf16[2048,1536]{1,0:T(8,128)(2,1)}, bf16[2048,1536]{1,0:T(8,128)(2,1)S(1)}, u32[]{:S(2)}) copy-start(bf16[2048,1536]{1,0:T(8,128)(2,1)S(1)} %get-tuple-element.29.local) | copy-start | bytes 18874372
  17.7 1.3 copy-start.3
  19.0 3.4 %copy-start.9 = (bf16[2,256,512]{2,1,0:T(8,128)(2,1)}, bf16[2,256,512]{2,1,0:T(8,128)(2,1)S(1)}, u32[]{:S(2)}) copy-start(bf16[2,256,512]{2,1,0:T(8,128)(2,1)S(1)} %collective-permute-done.left) | copy-start | bytes 1572868
  22.3 0.8 copy-start.10
  209.2 3.7 %copy-start.8 = (bf16[512,512]{1,0:T(8,128)(2,1)S(1)}, bf16[512,512]{1,0:T(8,128)(2,1)}, u32[]{:S(2)}) copy-start(bf16[512,512]{1,0:T(8,128)(2,1)} %get-tuple-element.46) | copy-start | bytes 1572868
  209.2 4.7 %copy-start.6 = (bf16[512,2048]{1,0:T(8,128)(2,1)S(1)}, bf16[512,2048]{1,0:T(8,128)(2,1)}, u32[]{:S(2)}) copy-start(bf16[512,2048]{1,0:T(8,128)(2,1)} %get-tuple-element.47) | copy-start | bytes 6291460
  214.0 2.5 %copy-start.5 = (bf16[2048,512]{1,0:T(8,128)(2,1)S(1)}, bf16[2048,512]{1,0:T(8,128)(2,1)}, u32[]{:S(2)}) copy-start(bf16[2048,512]{1,0:T(8,128)(2,1)} %get-tuple-element.48) | copy-start | bytes 6291460
  216.5 2.6 %copy-start.11 = (f32[16,512]{1,0:T(8,128)S(1)}, f32[16,512]{1,0:T(8,128)}, u32[]{:S(2)}) copy-start(f32[16,512]{1,0:T(8,128)} %get-tuple-element.49) | copy-start | bytes 98308
  216.5 3.2 %copy-start.7 = (bf16[2048,512]{1,0:T(8,128)(2,1)S(1)}, bf16[2048,512]{1,0:T(8,128)(2,1)}, u32[]{:S(2)}) copy-start(bf16[2048,512]{1,0:T(8,128)(2,1)} %get-tuple-element.44) | copy-start | bytes 6291460

commit v2 on v1

--- a/solution.py
+++ b/solution.py
@@ -15,10 +15,15 @@
 TILE = 256
 ENTRIES = 8
 BLOCK = 256
+MLP_BLOCK = 512
 PIECE = 512
 WINDOW = 64
 GROUPS = 2
-EVERY = 4
+MOVES = tuple(range(5, 36, 6))
+LATE = 2
+APART = 1
+AHEAD = 5
+BLOCKS_AHEAD = 3
 
 EPSILON = 1e-05
 NEGATIVE = -1e30
@@ -95,7 +100,7 @@
     zero = jnp.int32(0)
     for b in range(tiles[0]):
         table[base + b * ENTRIES] = 0
-    _, count, _, _, fitted_end = lax.fori_loop(0, slots, step, (zero, zero, zero, zero, zero))
+    _, count, _, _, fitted_end = lax.fori_loop(0, slots, step, (zero, zero, zero, zero, zero), unroll=5)
     table[base + tiles[0] * ENTRIES] = count
     table[base + tiles[0] * ENTRIES + 1] = fitted_end
     windows = local_len // WINDOW
@@ -131,36 +136,105 @@
     return one_hot, keys
 
 
-def project_kernel(tokens, w_qkv, gain, projected, normed_t):
+def project_kernel(
+    devices, local_len, tokens, w_qkv, gain, source, projected, normed_t, halo, zero, halo_sem, zero_sem
+):
+    step = pl.program_id(0)
+    rows = halo.shape[1]
+    seq = lax.axis_index("seq")
+    after, before = seq < devices[1] - 1, seq > 0
+
+    def halo_copy(side, row):
+        start = row * local_len + (local_len - HALO if side == 0 else 0)
+        return pltpu.make_async_remote_copy(
+            src_ref=source.at[start : start + HALO],
+            dst_ref=halo.at[side, row],
+            send_sem=halo_sem.at[0, side, row],
+            recv_sem=halo_sem.at[1, side, row],
+            device_id={"seq": seq + 1 if side == 0 else seq - 1},
+            device_id_type=MESH,
+        )
+
+    def fill(side, row):
+        return pltpu.make_async_copy(zero, halo.at[side, row], zero_sem.at[side, row])
+
+    sides = ((0, after, before), (1, before, after))
+
+    @pl.when(step == 0)
+    def _():
+        barrier = pltpu.get_barrier_semaphore()
+        for d in range(1, devices[1]):
+            peer = {"seq": lax.rem(seq + d, devices[1])}
+            pl.semaphore_signal(barrier, inc=1, device_id=peer, device_id_type=MESH)
+        zero[...] = jnp.zeros_like(zero)
+        pl.semaphore_wait(barrier, devices[1] - 1)
+        for side, sends, receives in sides:
+
+            @pl.when(sends)
+            def _():
+                for row in range(rows):
+                    halo_copy(side, row).start()
+
+            @pl.when(jnp.logical_not(receives))
+            def _():
+                for row in range(rows):
+                    fill(side, row).start()
+
     normed, _ = normalize(tokens[...].astype(F32))
     low = (normed * gain[...]).astype(BF16)
     normed_t[...] = low.T
     projected[...] = jnp.dot(low, w_qkv[...], preferred_element_type=F32).astype(BF16)
 
-
-def project(tokens, w_qkv, gain):
+    @pl.when(step == pl.num_programs(0) - 1)
+    def _():
+        for side, sends, receives in sides:
+
+            @pl.when(sends)
+            def _():
+                for row in range(rows):
+                    halo_copy(side, row).wait_send()
+
+            @pl.when(receives)
+            def _():
+                for row in range(rows):
+                    halo_copy(side, row).wait_recv()
+
+            @pl.when(jnp.logical_not(receives))
+            def _():
+                for row in range(rows):
+                    fill(side, row).wait()
+
+
+def project(devices, rows, tokens, w_qkv, gain):
     count, width = tokens.shape
     wide = w_qkv.shape[1]
-    block = 2 * BLOCK
+    block = BLOCK
+    dma = pltpu.SemaphoreType.DMA
     return pl.pallas_call(
-        project_kernel,
+        functools.partial(project_kernel, devices, count // rows),
         grid=(count // block,),
         out_shape=(
             jax.ShapeDtypeStruct((count, wide), BF16),
             jax.ShapeDtypeStruct((width, count), BF16),
+            jax.ShapeDtypeStruct((2, rows, HALO, width), BF16),
         ),
         in_specs=[
             pl.BlockSpec((block, width), lambda i: (i, 0)),
             whole_spec(width, wide),
             whole_spec(1, width),
+            pl.BlockSpec(memory_space=pl.ANY),
         ],
         out_specs=(
             pl.BlockSpec((block, wide), lambda i: (i, 0)),
             pl.BlockSpec((width, block), lambda i: (0, i)),
+            pl.BlockSpec(memory_space=pl.ANY),
         ),
-        compiler_params=pltpu.CompilerParams(vmem_limit_bytes=40 * MIB),
+        scratch_shapes=[pltpu.VMEM((HALO, width), BF16), dma((2, 2, rows)), dma((2, rows))],
+        compiler_params=pltpu.CompilerParams(
+            collective_id=1, has_side_effects=True, vmem_limit_bytes=60 * MIB
+        ),
         name="project",
-    )(tokens, w_qkv, gain)
+    )(tokens, w_qkv, gain, tokens)
 
 
 def attend_forward_kernel(
@@ -171,7 +245,7 @@
     local_len = local.shape[0]
     count = plan_tiles(lengths, table, row, tiles)
     for side, tokens in enumerate((left, right)):
-        normed = layer_norm(tokens[0].astype(F32), gain[...]).astype(BF16)
+        normed = layer_norm(tokens[0, 0].astype(F32), gain[...]).astype(BF16)
         made = jnp.dot(normed, w_qkv[...], preferred_element_type=F32).astype(BF16)
         start = side * (HALO + local_len)
         for c in range(12):
@@ -198,40 +272,55 @@
         hot[...] = one_hot
         for group in range(GROUPS):
             stage[slot, group, 8] = key_fill.astype(BF16)
-        for pair in range(4):
-            q = spread[pair, pl.ds(begin, TILE), :].astype(BF16)
-            k = spread[4 + pair, pl.ds(begin, TILE), :].astype(BF16)
-            v = spread[8 + pair, pl.ds(begin, TILE), :].astype(BF16)
+        loaded, held = {}, {}
+        key_fill = key_fill.astype(BF16)
+
+        def front(h):
+            pair, side = h // 2, h % 2
             group, i = pair // 2, pair % 2
-            stage[slot, group, i] = q
-            stage[slot, group, 2 + i] = k
-            stage[slot, group, 4 + i] = v
-            fill_q, fill_k = hot[...].astype(BF16), stage[slot, group, 8]
+            if side == 0:
+                loaded[pair] = tuple(spread[4 * n + pair, pl.ds(begin, TILE), :].astype(BF16) for n in range(3))
+                for n in range(3):
+                    stage[slot, group, 2 * n + i] = loaded[pair][n]
+            q, k, _ = loaded[pair]
+            own = low if side == 0 else ~low
+            return lax.dot_general(
+                jnp.where(own, q, hot[...].astype(BF16)),
+                jnp.where(own, k, key_fill),
+                NT,
+                preferred_element_type=F32,
+            )
+
+        def back(h, scores):
+            pair, side = h // 2, h % 2
+            v = loaded[pair][2]
             zero = jnp.zeros_like(v)
-            made, peaks = 0.0, []
-            for side in range(2):
-                own = low if side == 0 else ~low
-                scores = lax.dot_general(
-                    jnp.where(own, q, fill_q),
-                    jnp.where(own, k, fill_k),
-                    NT,
-                    preferred_element_type=F32,
-                )
-                peak = jnp.max(scores, axis=1, keepdims=True)
-                weights = jnp.exp2((scores - peak) * SCALE2).astype(BF16)
-                both = jnp.concatenate([jnp.where(own, v, zero), jnp.where(own, zero + 1, zero)], axis=1)
-                made += jnp.dot(weights, both, preferred_element_type=F32)
-                peaks.append(peak)
+            own = low if side == 0 else ~low
+            peak = jnp.max(scores, axis=1, keepdims=True)
+            weights = jnp.exp2((scores - peak) * SCALE2).astype(BF16)
+            both = jnp.concatenate([jnp.where(own, v, zero), jnp.where(own, zero + 1, zero)], axis=1)
+            made = jnp.dot(weights, both, preferred_element_type=F32)
+            if side == 0:
+                held[pair] = (made, peak)
+                return
+            made += held[pair][0]
             total = made[:, 128:]
             out[pair, pl.ds(begin, TILE), :] = made[:, :128] / total
             total = pltpu.roll(total, E, 1)
-            log_sum = jnp.where(low, peaks[1], peaks[0]) + jnp.log2(total) * (1.0 / SCALE2)
+            log_sum = jnp.where(low, peak, held[pair][1]) + jnp.log2(total) * (1.0 / SCALE2)
             first = log_sum.astype(BF16).astype(F32)
             rest = log_sum - first
             second = rest.astype(BF16).astype(F32)
             fill = jnp.where(place == 7, second - rest, hot[...])
             fill = jnp.where(place == 6, -second, fill)
-            stage[slot, group, 6 + i] = jnp.where(place == 5, -first, fill).astype(BF16)
+            stage[slot, pair // 2, 6 + pair % 2] = jnp.where(place == 5, -first, fill).astype(BF16)
+
+        ahead = front(0)
+        for h in range(8):
+            now = ahead
+            if h < 7:
+                ahead = front(h + 1)
+            back(h, now)
         store(slot, at).start()
         return 0
 
@@ -246,9 +335,9 @@
     store(lax.rem(count + 1, 2), row * tiles[0] + count - 1).wait()
 
 
-def attend_forward(lengths, local, left, right, w_qkv, gain):
+def attend_forward(lengths, local, halo, w_qkv, gain):
     rows = lengths.shape[0]
-    width = left.shape[2]
+    width = halo.shape[3]
     local_len = local.shape[0] // rows
     most = max_tiles(local_len)
     held = local_len + 2 * HALO
@@ -265,8 +354,8 @@
         in_specs=[
             smem_spec(),
             pl.BlockSpec((local_len, 3 * width), lambda r: (r, 0)),
-            row_spec(HALO, width),
-            row_spec(HALO, width),
+            pl.BlockSpec((1, 1, HALO, width), lambda r: (0, r, 0, 0)),
+            pl.BlockSpec((1, 1, HALO, width), lambda r: (1, r, 0, 0)),
             whole_spec(width, 3 * width),
             whole_spec(1, width),
         ],
@@ -282,9 +371,19 @@
             pltpu.VMEM((2, GROUPS, 9, TILE, 128), BF16),
             pltpu.SemaphoreType.DMA((2,)),
         ],
-        compiler_params=pltpu.CompilerParams(vmem_limit_bytes=56 * MIB),
+        compiler_params=pltpu.CompilerParams(vmem_limit_bytes=60 * MIB),
         name="attend_forward",
-    )(lengths, local, left, right, w_qkv, gain)
+    )(lengths, local, halo, halo, w_qkv, gain)
+
+
+def interleave(chains, lag):
+    live = {n: chain for n, chain in enumerate(chains)}
+    turn = 0
+    while live:
+        for n in list(live):
+            if turn >= n * lag and next(live[n], None) is None:
+                del live[n]
+        turn += 1
 
 
 def mlp_kernel(
@@ -297,58 +396,78 @@
     per_row = local_len // block
     row = step // per_row
     begin = lax.axis_index("seq") * local_len + (step % per_row) * block
-    positions = begin + lax.broadcasted_iota(jnp.int32, (block, 1), 0)
-    valid = positions < table[(row * (most + 1) + most) * ENTRIES + 1]
-    attn = jnp.dot(mixed[...], w_out[...], preferred_element_type=F32)
-    resid = tokens[...].astype(F32) + jnp.where(valid, attn, 0.0)
-    normed, scale = normalize(resid)
-    low = (normed * gain[...]).astype(BF16)
-    normed_t[...] = low.T
-    mixed_t[...] = mixed[...].T
-    dy = cotangent[...]
-    cotangent_t[...] = dy.T
-    piece = 512
-    dense, d_normed = resid, 0.0
-    for j in range(w_up.shape[1] // piece):
-        columns = slice(j * piece, (j + 1) * piece)
-        hidden = jnp.dot(low, w_up[:, columns], preferred_element_type=F32)
-        square = hidden * hidden
-        bent = jnp.tanh(hidden * (GELU_A + (GELU_A * GELU_B) * square))
-        half = 0.5 + 0.5 * bent
-        act = (hidden * half).astype(BF16)
-        slope = half + (0.5 - 0.5 * bent * bent) * hidden * (GELU_A + (3.0 * GELU_A * GELU_B) * square)
-        d_act = lax.dot_general(dy, w_down[columns, :], NT, preferred_element_type=F32)
-        grad = (d_act * slope).astype(BF16)
-        for part in range(piece // 256):
-            activated[j * (piece // 256) + part] = act[:, part * 256 : (part + 1) * 256]
-            d_hidden[j * (piece // 256) + part] = grad[:, part * 256 : (part + 1) * 256]
-        dense += jnp.dot(act, w_down[columns, :], preferred_element_type=F32)
-        d_normed += lax.dot_general(grad, w_up[:, columns], NT, preferred_element_type=F32)
-    output[...] = dense.astype(BF16)
+    fitted_end = table[(row * (most + 1) + most) * ENTRIES + 1]
+    piece = 256
+    pieces = w_up.shape[1] // piece
 
     @pl.when(step == 0)
     def _():
         grad_gain[...] = jnp.zeros_like(grad_gain)
 
-    grad_gain[...] += fold_rows(d_normed * normed)
-    made = dy.astype(F32) + normalize_back(d_normed * gain[...], normed, scale)
-    d_resid[...] = made
-    attn_low = jnp.where(valid, made, 0.0).astype(BF16)
-    for part in range(attn_low.shape[1] // 256):
-        d_attn[part] = attn_low[:, part * 256 : (part + 1) * 256]
-    d_mixed[...] = lax.dot_general(attn_low, w_out[...], NT, preferred_element_type=F32).astype(BF16)
+    def chain(first):
+        part = slice(first, first + BLOCK)
+        positions = begin + first + lax.broadcasted_iota(jnp.int32, (BLOCK, 1), 0)
+        valid = positions < fitted_end
+        attn = jnp.dot(mixed[part, :], w_out[...], preferred_element_type=F32)
+        dy = cotangent[part, :]
+        yield True
+        resid = tokens[part, :].astype(F32) + jnp.where(valid, attn, 0.0)
+        normed, scale = normalize(resid)
+        low = (normed * gain[...]).astype(BF16)
+        yield True
+
+        def front(j):
+            columns = slice(j * piece, (j + 1) * piece)
+            hidden = jnp.dot(low, w_up[:, columns], preferred_element_type=F32)
+            return hidden, lax.dot_general(dy, w_down[columns, :], NT, preferred_element_type=F32)
+
+        dense, d_normed = resid, 0.0
+        ahead = front(0)
+        for j in range(pieces):
+            columns = slice(j * piece, (j + 1) * piece)
+            hidden, d_act = ahead
+            if j + 1 < pieces:
+                ahead = front(j + 1)
+            square = hidden * hidden
+            bent = jnp.tanh(hidden * (GELU_A + (GELU_A * GELU_B) * square))
+            half = 0.5 + 0.5 * bent
+            act = (hidden * half).astype(BF16)
+            slope = half + (0.5 - 0.5 * bent * bent) * hidden * (GELU_A + (3.0 * GELU_A * GELU_B) * square)
+            grad = (d_act * slope).astype(BF16)
+            activated[j, part, :] = act
+            d_hidden[j, part, :] = grad
+            dense += jnp.dot(act, w_down[columns, :], preferred_element_type=F32)
+            d_normed += lax.dot_general(grad, w_up[:, columns], NT, preferred_element_type=F32)
+            if j == 1:
+                normed_t[:, part] = low.T
+            if j == 2:
+                mixed_t[:, part] = mixed[part, :].T
+            if j == 3:
+                cotangent_t[:, part] = dy.T
+            yield True
+        output[part, :] = dense.astype(BF16)
+        grad_gain[...] += fold_rows(d_normed * normed)
+        made = dy.astype(F32) + normalize_back(d_normed * gain[...], normed, scale)
+        yield True
+        d_resid[part, :] = made
+        attn_low = jnp.where(valid, made, 0.0).astype(BF16)
+        for n in range(attn_low.shape[1] // 256):
+            d_attn[n, part, :] = attn_low[:, n * 256 : (n + 1) * 256]
+        d_mixed[part, :] = lax.dot_general(attn_low, w_out[...], NT, preferred_element_type=F32).astype(BF16)
+
+    interleave([chain(first) for first in range(0, block, BLOCK)], 3)
 
 
 def mlp(local_len, table, tokens, mixed, cotangent, w_out, w_up, w_down, gain):
     count, width = tokens.shape
     hidden = w_up.shape[1]
-    rows_of = lambda w: pl.BlockSpec((BLOCK, w), lambda i: (i, 0))
-    blocks_of = lambda w: pl.BlockSpec((w // 256, BLOCK, 256), lambda i: (0, i, 0))
-    turned = pl.BlockSpec((width, BLOCK), lambda i: (0, i))
+    rows_of = lambda w: pl.BlockSpec((MLP_BLOCK, w), lambda i: (i, 0))
+    blocks_of = lambda w: pl.BlockSpec((w // 256, MLP_BLOCK, 256), lambda i: (0, i, 0))
+    turned = pl.BlockSpec((width, MLP_BLOCK), lambda i: (0, i))
     shape = jax.ShapeDtypeStruct
     return pl.pallas_call(
         functools.partial(mlp_kernel, (max_tiles(local_len), local_len)),
-        grid=(count // BLOCK,),
+        grid=(count // MLP_BLOCK,),
         out_shape=(
             shape((count, width), BF16),
             shape((hidden // 256, count, 256), BF16),
@@ -383,39 +502,57 @@
             turned,
             whole_spec(8, width),
         ),
-        compiler_params=pltpu.CompilerParams(vmem_limit_bytes=56 * MIB),
+        compiler_params=pltpu.CompilerParams(vmem_limit_bytes=60 * MIB),
         name="mlp",
     )(table, tokens, mixed, cotangent, w_out, w_up, w_down, gain)
 
 
 def tile_backward(pairs, packed, fills, grad_of, put):
     low = lax.broadcasted_iota(jnp.int32, (TILE, 128), 1) < E
-    for pair in range(pairs):
-        q, k, v, o = packed(pair), packed(pairs + pair), packed(2 * pairs + pair), grad_of(pair)
-        fill_q, fill_k = fills(pair), fills(pairs)
+    key_fill = fills(pairs)
+    loaded = {}
+
+    def front(h):
+        pair, side = h // 2, h % 2
+        if side == 0:
+            loaded[pair] = (packed(pair), packed(pairs + pair), packed(2 * pairs + pair), grad_of(pair), fills(pair))
+        q, k, v, o, fill = loaded[pair]
+        own = low if side == 0 else ~low
+        own_o = jnp.where(own, o, jnp.zeros_like(o))
+        scores = lax.dot_general(
+            jnp.where(own, k, key_fill), jnp.where(own, q, fill), NT, preferred_element_type=F32
+        )
+        d_probs = lax.dot_general(v, own_o, NT, preferred_element_type=F32)
+        return scores, d_probs, own_o
+
+    made = {}
+
+    def back(h, scores, d_probs, own_o):
+        pair, side = h // 2, h % 2
+        q, k, _, _, _ = loaded[pair]
+        own = low if side == 0 else ~low
         zero = jnp.zeros_like(q)
-        dq, dk, dv = 0.0, 0.0, 0.0
-        for side in range(2):
-            own = low if side == 0 else ~low
-            own_o = jnp.where(own, o, zero)
-            scores = lax.dot_general(
-                jnp.where(own, k, fill_k), jnp.where(own, q, fill_q), NT, preferred_element_type=F32
-            )
-            probs = jnp.exp2(scores * SCALE2)
-            d_probs = lax.dot_general(v, own_o, NT, preferred_element_type=F32)
-            weighted = probs * d_probs
-            inner = jnp.sum(weighted, axis=0, keepdims=True)
-            d_scores = (weighted - probs * inner).astype(BF16)
-            dq += lax.dot_general(d_scores, jnp.where(own, k, zero), TN, preferred_element_type=F32)
-            dk += jnp.dot(d_scores, jnp.where(own, q, zero), preferred_element_type=F32)
-            dv += jnp.dot(probs.astype(BF16), own_o, preferred_element_type=F32)
-        put(pair, dq * 0.125)
-        put(pairs + pair, dk * 0.125)
-        put(2 * pairs + pair, dv)
-
-
-def row_spec(*shape):
-    return pl.BlockSpec((1,) + shape, lambda r: (r,) + (0,) * len(shape))
+        probs = jnp.exp2(scores * SCALE2)
+        weighted = probs * d_probs
+        inner = jnp.sum(weighted, axis=0, keepdims=True)
+        d_scores = (weighted - probs * inner).astype(BF16)
+        dv = jnp.dot(probs.astype(BF16), own_o, preferred_element_type=F32)
+        dk = jnp.dot(d_scores, jnp.where(own, q, zero), preferred_element_type=F32)
+        dq = lax.dot_general(d_scores, jnp.where(own, k, zero), TN, preferred_element_type=F32)
+        if side == 0:
+            made[pair] = (dq, dk, dv)
+        else:
+            first = made[pair]
+            put(pair, (first[0] + dq) * 0.125)
+            put(pairs + pair, (first[1] + dk) * 0.125)
+            put(2 * pairs + pair, first[2] + dv)
+
+    ahead = front(0)
+    for h in range(2 * pairs):
+        now = ahead
+        if h + 1 < 2 * pairs:
+            ahead = front(h + 1)
+        back(h, *now)
 
 
 def whole_spec(*shape):
@@ -426,18 +563,17 @@
     return pl.BlockSpec(memory_space=pltpu.SMEM)
 
 
-def exchange(values, devices):
-    before = lax.ppermute(values[:, -HALO:], "seq", [(i, i + 1) for i in range(devices - 1)])
-    after = lax.ppermute(values[:, :HALO], "seq", [(i + 1, i) for i in range(devices - 1)])
-    return before, after
-
-
 def sum_plan(devices):
     dp, seq = devices
-    chip = [("dp", 1 << b) for b in range(1, dp.bit_length() - 1)]
-    core = [("dp", 1)]
-    along = [("seq", 1 << b) for b in range(seq.bit_length() - 1)]
-    return [core + chip + along, core + chip[::-1] + along]
+    chip = [1 << b for b in range(1, dp.bit_length() - 1)]
+    along = [1 << b for b in range(seq.bit_length() - 1)]
+
+    def paired(axis, bits):
+        return [(axis, tuple(bits[n : n + 2])) for n in range(0, len(bits), 2)]
+
+    core, z = [("dp", (1,))], paired("seq", along)
+    one = [("dp", (bit,)) for bit in chip]
+    return [core + one + z, core + one[::-1] + z, core + paired("dp", chip) + z]
 
 
 def chunk_pieces(devices):
@@ -450,95 +586,133 @@
 class GradSum:
     def __init__(self, devices, work, slots, done, send_sem, recv_sem):
         self.plans = sum_plan(devices)
-        self.steps = len(self.plans[0])
         self.work, self.slots, self.done = work, slots, done
         self.send_sem, self.recv_sem = send_sem, recv_sem
         self.here = {"dp": lax.axis_index("dp"), "seq": lax.axis_index("seq")}
         self.sizes = chunk_pieces(devices)
         self.paths, self.active = [], []
+        self.queue, self.clock, self.free_at = [], 0, 0
         base = 0
         for chunk, pieces in enumerate(self.sizes):
             offset, rows, slot, path = base, pieces * PIECE, base, []
-            for axis, bit in self.plan(chunk):
-                mine, _ = self.other(axis, bit)
-                rows //= 2
-                keep, give = offset + mine * rows, offset + (1 - mine) * rows
-                path.append((keep, give, slot, rows))
-                offset, slot = keep, slot + rows
+            for axis, bits in self.plan(chunk):
+                mine, others = self.peers(axis, bits)
+                rows //= 1 << len(bits)
+                keep = offset + mine * rows
+                path.append((keep, [offset + n * rows for n, _ in others], slot, rows))
+                offset, slot = keep, slot + rows * len(others)
             self.paths.append(path)
             base += pieces * PIECE
 
     def plan(self, chunk):
-        return self.plans[chunk % 2]
-
-    def other(self, axis, bit):
-        mine = (self.here[axis] // bit) % 2
-        return mine, {axis: self.here[axis] + bit - 2 * bit * mine}
-
-    def copy(self, chunk, t, source, target, to):
-        return pltpu.make_async_remote_copy(
-            src_ref=source,
-            dst_ref=target,
-            send_sem=self.send_sem.at[chunk, t],
-            recv_sem=self.recv_sem.at[chunk, t],
-            device_id=self.other(*to)[1],
-            device_id_type=MESH,
+        return self.plans[2 if chunk >= len(self.sizes) - LATE else chunk % 2]
+
+    def peers(self, axis, bits):
+        index = self.here[axis]
+        own = [(index // bit) % 2 for bit in bits]
+        others = []
+        for mask in range(1, 1 << len(bits)):
+            number, to = 0, index
+            for i, bit in enumerate(bits):
+                flip = (mask >> i) % 2
+                number = number + (1 - own[i] if flip else own[i]) * (1 << i)
+                to = to + flip * (bit - 2 * bit * own[i])
+            others.append((number, {axis: to}))
+        return sum(own[i] * (1 << i) for i in range(len(bits))), others
+
+    def copies(self, chunk, t, pairs):
+        axis, bits = self.plan(chunk)[min(t, 2 * len(self.plan(chunk)) - 1 - t)]
+        return [
+            pltpu.make_async_remote_copy(
+                src_ref=source,
+                dst_ref=target,
+                send_sem=self.send_sem.at[chunk, t, n],
+                recv_sem=self.recv_sem.at[chunk, t, n],
+                device_id=to,
+                device_id_type=MESH,
+            )
+            for n, ((source, target), (_, to)) in enumerate(zip(pairs, self.peers(axis, bits)[1]))
+        ]
+
+    def spreading(self, chunk, s):
+        _, gives, slot, rows = self.paths[chunk][s]
+        return self.copies(
+            chunk,
+            s,
+            [
+                (
+                    self.work.at[pl.ds(pl.multiple_of(give, 16), rows)],
+                    self.slots.at[slot + n * rows : slot + (n + 1) * rows],
+                )
+                for n, give in enumerate(gives)
+            ],
         )
 
-    def halving(self, chunk, s):
-        _, give, slot, rows = self.paths[chunk][s]
-        source = self.work.at[pl.ds(pl.multiple_of(give, 16), rows)]
-        return self.copy(chunk, s, source, self.slots.at[slot : slot + rows], self.plan(chunk)[s])
-
-    def doubling(self, chunk, s, received):
-        keep, give, _, rows = self.paths[chunk][s]
-        part = self.done.at[pl.ds(pl.multiple_of(give if received else keep, 16), rows)]
-        return self.copy(chunk, self.steps + s, part, part, self.plan(chunk)[s])
+    def gathering(self, chunk, s, received):
+        keep, gives, _, rows = self.paths[chunk][s]
+        parts = [
+            self.done.at[pl.ds(pl.multiple_of(give if received else keep, 16), rows)] for give in gives
+        ]
+        return self.copies(chunk, 2 * len(self.plan(chunk)) - 1 - s, [(part, part) for part in parts])
 
     def add(self, chunk, s):
-        keep, _, slot, rows = self.paths[chunk][s]
-        into = self.done if s + 1 == self.steps else self.work
+        keep, gives, slot, rows = self.paths[chunk][s]
+        into = self.done if s + 1 == len(self.plan(chunk)) else self.work
         count = next(n for n in range(1, rows) if rows % (16 * n) == 0 and rows // n <= 512)
         block = rows // count
 
         @pl.loop(0, count)
         def _(i):
             at = pl.ds(pl.multiple_of(keep + i * block, 16), block)
-            theirs = self.slots[pl.ds(pl.multiple_of(slot + i * block, 16), block), :]
-            into[at, :] = (self.work[at, :].astype(F32) + theirs.astype(F32)).astype(BF16)
+            total = self.work[at, :].astype(F32)
+            for n in range(len(gives)):
+                from_at = pl.ds(pl.multiple_of(slot + n * rows + i * block, 16), block)
+                total += self.slots[from_at, :].astype(F32)
+            into[at, :] = total.astype(BF16)
 
     def event(self, chunk, t):
-        steps = self.steps
+        steps = len(self.plan(chunk))
         if 0 < t <= steps:
-            self.halving(chunk, t - 1).wait()
+            for copy in self.spreading(chunk, t - 1):
+                copy.wait()
             self.add(chunk, t - 1)
         elif t > steps:
-            self.doubling(chunk, 2 * steps - t, False).wait_send()
-            self.doubling(chunk, 2 * steps - t, True).wait_recv()
+            for copy in self.gathering(chunk, 2 * steps - t, False):
+                copy.wait_send()
+            for copy in self.gathering(chunk, 2 * steps - t, True):
+                copy.wait_recv()
         if t < steps:
-            self.halving(chunk, t).start()
+            for copy in self.spreading(chunk, t):
+                copy.start()
         elif t < 2 * steps:
-            self.doubling(chunk, 2 * steps - 1 - t, False).start()
+            for copy in self.gathering(chunk, 2 * steps - 1 - t, False):
+                copy.start()
         return t == 2 * steps
 
-    def begin(self, chunks):
-        for chunk in chunks:
-            self.event(chunk, 0)
-            self.active.append([chunk, 1])
+    def begin(self, chunks, now=False):
+        self.queue += chunks
+        while self.queue and (now or self.clock >= self.free_at):
+            for chunk in self.queue[:2]:
+                self.event(chunk, 0)
+                self.active.append([chunk, 1])
+            self.queue = self.queue[2:]
+            self.free_at = self.clock + APART
 
     def advance(self, finish):
+        self.clock += 1
         for entry in list(self.active):
             if self.event(*entry):
                 finish(entry[0])
                 self.active.remove(entry)
             entry[1] += 1
+        self.begin([])
 
 
 def backward_kernel(
     devices, tiles, table, gains, w_qkv, gain_one,
     normed_two_t, cotangent_t, mixed_t, normed_one_t, d_hidden, activated, d_attn, d_mixed, tokens, d_resid,
     packed,
-    grad_tokens, grad_qkv, grad_out, grad_up, grad_down, gains_out,
+    grad_tokens, summed, gains_out,
     work, slots, done, left_a, left_b, right_block, halo, d_mix, tok, resid, made_tok, d_proj, bins, d_out,
     tile_in, gain_slots, gain_one_sum,
     send_sem, recv_sem, gain_send, gain_recv, halo_sem, load_sem, block_sem, tile_sem, store_sem, out_sem,
@@ -548,11 +722,10 @@
     rows = count // local_len
     seq = lax.axis_index("seq")
     sums = GradSum(devices, work, slots, done, send_sem, recv_sem)
-    steps = sums.steps
 
     barrier = pltpu.get_barrier_semaphore()
     after, before = seq < devices[1] - 1, seq > 0
-    peers = [sums.other(axis, bit)[1] for axis, bit in sums.plans[0] if axis == "dp"]
+    peers = [to for axis, bits in sums.plans[2] if axis == "dp" for _, to in sums.peers(axis, bits)[1]]
     peers += [{"seq": lax.rem(seq + d, devices[1])} for d in range(1, devices[1])]
     for peer in peers:
         pl.semaphore_signal(barrier, inc=1, device_id=peer, device_id_type=MESH)
@@ -566,8 +739,8 @@
     load_tok = pltpu.make_async_copy(tokens, tok, load_sem.at[5])
     load_resid = pltpu.make_async_copy(d_resid, resid, load_sem.at[6])
     load_a(normed_two_t, 0).start()
-    load_block(d_hidden, 0, 0).start()
-    load_block(d_hidden, 1, 1).start()
+    for n in range(BLOCKS_AHEAD):
+        load_block(d_hidden, n, n).start()
     load_b(cotangent_t, 1).start()
     load_mix.start()
 
@@ -596,25 +769,15 @@
             for row in range(rows):
                 halo[side, row] = jnp.zeros(halo.shape[2:], BF16)
 
-    homes = [(grad_up, 0, c) for c in range(16)]
-    homes += [(grad_down, i * PIECE, c) for i in range(4) for c in range(4)]
-    homes += [(grad_out, 0, c) for c in range(4)]
-    homes += [(grad_qkv, 0, kind * 4 + 2 * g + i) for g in range(GROUPS) for kind in range(3) for i in range(2)]
     stored = []
 
-    def store(piece):
-        ref, row, c = homes[piece]
-        return pltpu.make_async_copy(
-            done.at[piece * PIECE : (piece + 1) * PIECE],
-            ref.at[row : row + PIECE, c * 128 : (c + 1) * 128],
-            out_sem.at[piece],
-        )
+    def store(chunk):
+        part = pl.ds(sum(sums.sizes[:chunk]) * PIECE, sums.sizes[chunk] * PIECE)
+        return pltpu.make_async_copy(done.at[part], summed.at[part], out_sem.at[chunk])
 
     def finish(chunk):
-        first = sum(sums.sizes[:chunk])
-        for piece in range(first, first + sums.sizes[chunk]):
-            store(piece).start()
-            stored.append(piece)
+        store(chunk).start()
+        stored.append(chunk)
 
     begun = [0]
 
@@ -623,7 +786,7 @@
         while begun[0] < len(sums.sizes) and sum(sums.sizes[: begun[0] + 1]) <= pieces:
             chunks.append(begun[0])
             begun[0] += 1
-        sums.begin(chunks)
+        sums.begin(chunks, pieces >= 48)
 
     def put_columns(base, block, product):
         low = product.astype(BF16)
@@ -651,19 +814,18 @@
         if n in waits:
             waits[n].wait()
 
-        def one_block(j, _, n=n, lhs=lhs, ref=ref, first=first, blocks=blocks, base=base, put=put, at=at):
-            slot, later = lax.rem(at + j, 3), lax.rem(at + j + 2, 3)
+        upcoming = [(run[1], run[2], run[3]) for run in runs[n:]][:3]
+
+        def one_block(j, _, n=n, upcoming=upcoming, lhs=lhs, ref=ref, first=first, blocks=blocks, base=base, put=put, at=at):
+            slot, later = lax.rem(at + j, BLOCKS_AHEAD + 1), lax.rem(at + j + BLOCKS_AHEAD, BLOCKS_AHEAD + 1)
             load_block(ref, first + j, slot).wait()
-
-            @pl.when(j + 2 < blocks)
-            def _():
-                load_block(ref, first + j + 2, later).start()
-
-            if n + 1 < len(runs):
-
-                @pl.when(j + 2 >= blocks)
+            until = 0
+            for next_ref, next_first, next_blocks in upcoming:
+                since, until = until, until + next_blocks
+
+                @pl.when((j + BLOCKS_AHEAD >= since) & (j + BLOCKS_AHEAD < until))
                 def _():
-                    load_block(runs[n + 1][1], runs[n + 1][2] + j + 2 - blocks, later).start()
+                    load_block(next_ref, next_first + j + BLOCKS_AHEAD - since, later).start()
 
             put(base, first + j, jnp.dot(lhs[...], right_block[slot], preferred_element_type=F32))
             return 0
@@ -690,7 +852,8 @@
         group, spot = step // per_group, lax.rem(step, per_group)
         return pltpu.make_async_copy(packed.at[spot, group], tile_in.at[slot], tile_sem.at[slot])
 
-    load_tile(0, 0).start()
+    for n in range(AHEAD):
+        load_tile(n, n).start()
     load_mix.wait()
     for side, sends, receives in ((0, after, before), (1, before, after)):
 
@@ -705,14 +868,14 @@
                 halo_copy(side, row).wait_recv()
 
     def one_tile(step, _):
-        slot = lax.rem(step, 2)
+        slot = lax.rem(step, AHEAD + 1)
         group, spot = step // per_group, lax.rem(step, per_group)
         row, b = spot // most, lax.rem(spot, most)
         load_tile(step, slot).wait()
 
-        @pl.when(step + 1 < total)
+        @pl.when(step + AHEAD < total)
         def _():
-            load_tile(step + 1, 1 - slot).start()
+            load_tile(step + AHEAD, lax.rem(step + AHEAD, AHEAD + 1)).start()
 
         @pl.when(b == 0)
         def _():
@@ -760,7 +923,7 @@
 
         for k in range(total):
             ends_group = (k + 1) % per_group == 0
-            moves = k % EVERY == EVERY - 1 and sums.active
+            moves = k in MOVES and sums.active
             if not (ends_group or moves):
                 continue
 
@@ -808,35 +971,44 @@
 
     lax.fori_loop(0, blocks, input_block, 0)
 
-    def gain_copy(s):
-        return pltpu.make_async_remote_copy(
-            src_ref=gain_slots.at[2 * s],
-            dst_ref=gain_slots.at[2 * s + 1],
-            send_sem=gain_send.at[s],
-            recv_sem=gain_recv.at[s],
-            device_id=sums.other(*sums.plans[0][s])[1],
-            device_id_type=MESH,
-        )
-
-    gain_slots[0, :8] = gain_one_sum[...]
-    gain_slots[0, 8:] = gains[...]
-    gain_copy(0).start()
-    for s in range(steps):
+    gain_plan = sums.plans[2]
+
+    def gain_copies(s):
+        return [
+            pltpu.make_async_remote_copy(
+                src_ref=gain_slots.at[s, 0],
+                dst_ref=gain_slots.at[s, n + 1],
+                send_sem=gain_send.at[s, n],
+                recv_sem=gain_recv.at[s, n],
+                device_id=to,
+                device_id_type=MESH,
+            )
+            for n, (_, to) in enumerate(sums.peers(*gain_plan[s])[1])
+        ]
+
+    gain_slots[0, 0, :8] = gain_one_sum[...]
+    gain_slots[0, 0, 8:] = gains[...]
+    for copy in gain_copies(0):
+        copy.start()
+    for s in range(len(gain_plan)):
         if sums.active:
             sums.advance(finish)
-        gain_copy(s).wait()
-        joined = gain_slots[2 * s] + gain_slots[2 * s + 1]
-        if s + 1 < steps:
-            gain_slots[2 * s + 2] = joined
-            gain_copy(s + 1).start()
+        joined = gain_slots[s, 0]
+        for n, copy in enumerate(gain_copies(s)):
+            copy.wait()
+            joined += gain_slots[s, n + 1]
+        if s + 1 < len(gain_plan):
+            gain_slots[s + 1, 0] = joined
+            for copy in gain_copies(s + 1):
+                copy.start()
         else:
             gains_out[...] = joined
     while sums.active:
         sums.advance(finish)
     for i in range(blocks):
         store_tok(i).wait()
-    for piece in stored:
-        store(piece).wait()
+    for chunk in stored:
+        store(chunk).wait()
 
 
 def backward(
@@ -847,8 +1019,7 @@
     local_len = count // rows
     most = max_tiles(local_len)
     held = local_len + 2 * HALO
-    hidden, wide = d_hidden.shape[0] * d_hidden.shape[2], w_qkv.shape[1]
-    steps = len(sum_plan(devices)[0])
+    steps = max(len(plan) for plan in sum_plan(devices))
     chunks = len(chunk_pieces(devices))
     shape = jax.ShapeDtypeStruct
     anywhere = pl.BlockSpec(memory_space=pl.ANY)
@@ -858,21 +1029,18 @@
         functools.partial(backward_kernel, devices, (most, local_len)),
         out_shape=(
             shape((count, width), BF16),
-            shape((width, wide), BF16),
-            shape((width, width), BF16),
-            shape((width, hidden), BF16),
-            shape((hidden, width), BF16),
+            shape((48 * PIECE, 128), BF16),
             shape((16, width), F32),
         ),
         in_specs=[smem_spec(), vmem, vmem, vmem] + [anywhere] * 11,
-        out_specs=(anywhere,) * 5 + (vmem,),
+        out_specs=(anywhere, anywhere, vmem),
         scratch_shapes=[
             pltpu.VMEM((48 * PIECE, 128), BF16),
             pltpu.VMEM((48 * PIECE, 128), BF16),
             pltpu.VMEM((48 * PIECE, 128), BF16),
             pltpu.VMEM((width, count), BF16),
             pltpu.VMEM((width, count), BF16),
-            pltpu.VMEM((3, count, 256), BF16),
+            pltpu.VMEM((BLOCKS_AHEAD + 1, count, 256), BF16),
             pltpu.VMEM((2, rows, HALO, width), BF16),
             pltpu.VMEM((count, width), BF16),
             pltpu.VMEM((count, width), BF16),
@@ -881,19 +1049,19 @@
             pltpu.VMEM((12, count, 128), BF16),
             pltpu.VMEM((6, most * TILE + WINDOW, 128), F32),
             pltpu.VMEM((2, held, 128), F32),
-            pltpu.VMEM((2, 9, TILE, 128), BF16),
-            pltpu.VMEM((2 * steps, 16, width), F32),
+            pltpu.VMEM((AHEAD + 1, 9, TILE, 128), BF16),
+            pltpu.VMEM((steps, 4, 16, width), F32),
             pltpu.VMEM((8, width), F32),
-            dma((chunks, 2 * steps)),
-            dma((chunks, 2 * steps)),
-            dma((steps,)),
-            dma((steps,)),
+            dma((chunks, 2 * steps, 3)),
+            dma((chunks, 2 * steps, 3)),
+            dma((steps, 3)),
+            dma((steps, 3)),
             dma((2, 2, rows)),
             dma((7,)),
-            dma((3,)),
-            dma((2,)),
+            dma((BLOCKS_AHEAD + 1,)),
+            dma((AHEAD + 1,)),
             dma((count // BLOCK,)),
-            dma((48,)),
+            dma((chunks,)),
         ],
         compiler_params=pltpu.CompilerParams(
             collective_id=0, has_side_effects=True, vmem_limit_bytes=60 * MIB
@@ -905,6 +1073,55 @@
     )
 
 
+def unpack_kernel(up, down, out, *refs):
+    grad_qkv, grad_out, grad_up, grad_down = refs[3:]
+    for c in range(4):
+        columns = slice(c * 128, (c + 1) * 128)
+        grad_up[:, columns] = up[c].astype(F32)
+        grad_down[:, columns] = down[c].astype(F32)
+    grad_out[...] = out[0].astype(F32)
+    for n in range(3):
+        grad_qkv[:, n * 128 : (n + 1) * 128] = refs[n][0].astype(F32)
+
+
+def unpack(summed, width, hidden, wide):
+    pieces = summed.reshape(48, PIECE, 128)
+
+    def qkv_piece(n):
+        def place(i, k):
+            block = 3 * i + n
+            kind, pair = block // 4, block % 4
+            return (36 + 6 * (pair // 2) + 2 * kind + pair % 2, k, 0)
+
+        return pl.BlockSpec((1, PIECE // 2, 128), place)
+
+    shape = jax.ShapeDtypeStruct
+    return pl.pallas_call(
+        unpack_kernel,
+        grid=(4, 2),
+        out_shape=(
+            shape((width, wide), F32),
+            shape((width, width), F32),
+            shape((width, hidden), F32),
+            shape((hidden, width), F32),
+        ),
+        in_specs=[
+            pl.BlockSpec((4, PIECE // 2, 128), lambda i, k: (i, k, 0)),
+            pl.BlockSpec((4, PIECE // 2, 128), lambda i, k: (4 + i, k, 0)),
+            pl.BlockSpec((1, PIECE // 2, 128), lambda i, k: (32 + i, k, 0)),
+        ]
+        + [qkv_piece(n) for n in range(3)],
+        out_specs=(
+            pl.BlockSpec((width // 2, wide // 4), lambda i, k: (k, i)),
+            pl.BlockSpec((width // 2, width // 4), lambda i, k: (k, i)),
+            pl.BlockSpec((width // 2, hidden // 4), lambda i, k: (k, i)),
+            pl.BlockSpec((hidden // 8, width), lambda i, k: (2 * i + k, 0)),
+        ),
+        compiler_params=pltpu.CompilerParams(vmem_limit_bytes=60 * MIB),
+        name="unpack",
+    )(*[pieces] * 6)
+
+
 def body(
     devices, tokens, item_lengths, w_qkv, w_out, w_up, w_down, gain_one, gain_two, cotangent
 ):
@@ -912,18 +1129,16 @@
     count = rows * local_len
     gain_one, gain_two = gain_one.reshape(1, width), gain_two.reshape(1, width)
     flat = tokens.reshape(count, width)
-    left, right = exchange(tokens, devices[1])
-    projected, normed_one_t = project(flat, w_qkv, gain_one)
-    mixed, packed, table = attend_forward(item_lengths, projected, left, right, w_qkv, gain_one)
+    projected, normed_one_t, halo = project(devices, rows, flat, w_qkv, gain_one)
+    mixed, packed, table = attend_forward(item_lengths, projected, halo, w_qkv, gain_one)
     (
         output, activated, d_hidden, d_resid, d_attn, d_mixed, normed_two_t, mixed_t, cotangent_t, grad_gain_two
     ) = mlp(local_len, table, flat, mixed, cotangent.reshape(count, width), w_out, w_up, w_down, gain_two)
-    grad_tokens, grad_qkv, grad_out, grad_up, grad_down, gains = backward(
+    grad_tokens, summed, gains = backward(
         devices, rows, table, grad_gain_two, w_qkv, gain_one, normed_two_t, cotangent_t, mixed_t, normed_one_t,
         d_hidden, activated, d_attn, d_mixed, flat, d_resid, packed,
     )
-    summed = (grad_qkv, grad_out, grad_up, grad_down)
-    grads = tuple(g.astype(F32) for g in summed)
+    grads = tuple(unpack(summed, width, w_up.shape[1], w_qkv.shape[1]))
     gains = jnp.sum(gains.reshape(2, 8, width), axis=1)
     placed = (output.reshape(tokens.shape), grad_tokens.reshape(tokens.shape))
     return placed + grads + (gains[0], gains[1])

time: 221 us -> 205 us (0.928)
  Pallas kernels: 191 us -> 202 us
  other arithmetic: 9.9 us -> 0.02 us
  local copies, waits for them, and re-layouts: 9.52 us -> 1.92 us
  starting transfers between devices: 6.25 us -> 0 us
  waiting for transfers between devices: 3.36 us -> 0 us
    pallas_call x1 -> x2, Pallas kernels: 5.21 us -> 29.4 us  [the longest x1 20.2 us: project(): pl.pallas_call(functools.partial(project_kernel, devices, count // rows),...]
    convert_element_type x4 -> x0, other arithmetic: 9.88 us -> none  [body(): grads = tuple((g.astype(F32) for g in summed))]
    pallas_call x1, Pallas kernels: 126 us -> 117 us  [backward(): pl.pallas_call(functools.partial(backward_kernel, devices, (most, local_l...]
    ppermute x2 -> x0, starting transfers between devices: 6.25 us -> none  [the longest x1 4.96 us: exchange(): lax.ppermute(values[:, -HALO:], 'seq', [(i, i + 1) for i in range(devices...]
    unnamed x25 -> x5, local copies, waits for them, and re-layouts: 7.51 us -> 1.33 us
    pallas_call x1, Pallas kernels: 36.2 us -> 31.6 us  [mlp(): pl.pallas_call(functools.partial(mlp_kernel, (max_tiles(local_len), local...]
    ppermute x2 -> x0, waiting for transfers between devices: 3.36 us -> none  [the longest x1 3.36 us: exchange(): lax.ppermute(values[:, :HALO], 'seq', [(i + 1, i) for i in range(devices...]
  transfers between devices with their start and end apart: 2 -> 0, of which waited for: 1 -> 0; matrix products, arithmetic and copies ran while one was open for 0% -> 0% of each run, Pallas kernels for 2% -> 0%
where the time goes in v2:
time: 205 us
  Pallas kernels  202 us (99%)
    pallas_call x1, Pallas kernels, backward(): pl.pallas_call(functools.partial(backward_kernel, devices, (most, local_l...  117 us
    pallas_call x1, Pallas kernels, mlp(): pl.pallas_call(functools.partial(mlp_kernel, (max_tiles(local_len), local...  31.6 us
    pallas_call x1, Pallas kernels, attend_forward(): pl.pallas_call(functools.partial(attend_forward_kernel, (most, local_len,...  23.6 us
    pallas_call x1, Pallas kernels, project(): pl.pallas_call(functools.partial(project_kernel, devices, count // rows),...  20.2 us
    pallas_call x1, Pallas kernels, unpack(): pl.pallas_call(unpack_kernel, grid=(4, 2), out_shape=(shape((width, wide)...  9.16 us

profile of v2, /device:TPU:0, one launch (start us, length us, event | category | flops | bytes accessed | tf_op | source)
XLA Modules:
  0.0 204.5 jit_solution(3020007028319809479)
XLA Ops:
  0.6 20.2 %project.1 = (bf16[2048,1536]{1,0:T(8,128)(2,1)}, bf16[512,2048]{1,0:T(8,128)(2,1)}, bf16[2,2,256,512]{3,2,1,0:T(8,128)(2,1)}) custom-call(bf16[2048,512]{1,0:T(8,128)(2,1)} %bitcast.17, bf16[512,1536]{1,0:T(8,128)(2,1)} %w_qkv.5, f32[1,512]{1,0:T(1,128)} %bitcast.23, bf16[2048,512]{1,0:T(8,128)(2,1)} %bitcast.18), custom_call_target="tpu_custom_call" | custom-call | tf_op jit(solution)/shard_map/project/pallas_call | solution.py:213
  20.9 23.6 %attend_forward.1 = (bf16[2048,512]{1,0:T(8,128)(2,1)}, bf16[18,2,9,256,128]{4,3,2,1,0:T(8,128)(2,1)}, s32[288]{0:T(512)}) custom-call(s32[2,65]{1,0:T(2,128)} %lengths.1, bf16[2048,1536]{1,0:T(8,128)(2,1)} %get-tuple-element.31.local, bf16[2,2,256,512]{3,2,1,0:T(8,128)(2,1)} %get-tuple-element.32.left.right, ...), custom_call_target="tpu_custom_call" | custom-call | tf_op jit(solution)/shard_map/attend_forward/pallas_call | solution.py:344
  44.5 31.6 %mlp.1 = (bf16[2048,512]{1,0:T(8,128)(2,1)}, bf16[8,2048,256]{2,1,0:T(8,128)(2,1)}, bf16[8,2048,256]{2,1,0:T(8,128)(2,1)}, f32[2048,512]{1,0:T(8,128)}, bf16[2,2...) custom-call(s32[288]{0:T(512)} %get-tuple-element.33.table, ...), custom_call_target="tpu_custom_call" | custom-call | tf_op jit(solution)/shard_map/mlp/pallas_call | solution.py:468
  76.1 117.3 %backward.1 = (bf16[2048,512]{1,0:T(8,128)(2,1)}, bf16[24576,128]{1,0:T(8,128)(2,1)}, f32[16,512]{1,0:T(8,128)}) custom-call(s32[288]{0:T(512)} %get-tuple-element.33.table, f32[8,512]{1,0:T(8,128)} %get-tuple-element.36.gains, bf16[512,1536]{1,0:T(8,128)(2,1)} %w_qkv.5, f32[1,512]{1,0:T(1,128)} %bitcast.25, ...), custom_call_target="tpu_custom_call" | custom-call | tf_op jit(solution)/shard_map/backward/pallas_call | solution.py:1028
  193.4 0.0 copy-start.1
  193.4 0.0 copy-start
  193.4 9.2 %unpack.1 = (f32[512,1536]{1,0:T(8,128)}, f32[512,512]{1,0:T(8,128)}, f32[512,2048]{1,0:T(8,128)}, f32[2048,512]{1,0:T(8,128)}) custom-call(bf16[48,512,128]{2,1,0:T(8,128)(2,1)} %bitcast.11, bf16[48,512,128]{2,1,0:T(8,128)(2,1)} %bitcast.12, bf16[48,512,128]{2,1,0:T(8,128)(2,1)} %bitcast.13, bf16[48,512,128]{2,1,0:T(8,128)(2,1)} %bitcast.14, ...), custom_call_target="tpu_custom_call" | custom-call | tf_op jit(solution)/shard_map/unpack/pallas_call | solution.py:1099
  202.6 0.0 copy-done.1
  202.6 0.6 fusion
  203.2 0.0 copy-done
  203.2 1.3 copy.18
  (1 shorter events, 0.0 us)
Async XLA Ops:
  193.4 9.2 %copy-start.1 = (f32[16,512]{1,0:T(8,128)S(1)}, f32[16,512]{1,0:T(8,128)}, u32[]{:S(2)}) copy-start(f32[16,512]{1,0:T(8,128)} %get-tuple-element.53) | copy-start | bytes 98308
  193.4 9.8 %copy-start = (bf16[2048,512]{1,0:T(8,128)(2,1)S(1)}, bf16[2048,512]{1,0:T(8,128)(2,1)}, u32[]{:S(2)}) copy-start(bf16[2048,512]{1,0:T(8,128)(2,1)} %get-tuple-element.47) | copy-start | bytes 6291460

commit v3 on v2

--- a/solution.py
+++ b/solution.py
@@ -19,7 +19,7 @@
 PIECE = 512
 WINDOW = 64
 GROUPS = 2
-MOVES = tuple(range(5, 36, 6))
+MOVES = (6, 13, 20, 27, 34)
 LATE = 2
 APART = 1
 AHEAD = 5
@@ -299,11 +299,14 @@
             peak = jnp.max(scores, axis=1, keepdims=True)
             weights = jnp.exp2((scores - peak) * SCALE2).astype(BF16)
             both = jnp.concatenate([jnp.where(own, v, zero), jnp.where(own, zero + 1, zero)], axis=1)
-            made = jnp.dot(weights, both, preferred_element_type=F32)
             if side == 0:
-                held[pair] = (made, peak)
+                held[pair] = ((weights, both), peak)
                 return
-            made += held[pair][0]
+            made = jnp.dot(
+                jnp.concatenate([held[pair][0][0], weights], axis=1),
+                jnp.concatenate([held[pair][0][1], both], axis=0),
+                preferred_element_type=F32,
+            )
             total = made[:, 128:]
             out[pair, pl.ds(begin, TILE), :] = made[:, :128] / total
             total = pltpu.roll(total, E, 1)
@@ -315,11 +318,11 @@
             fill = jnp.where(place == 6, -second, fill)
             stage[slot, pair // 2, 6 + pair % 2] = jnp.where(place == 5, -first, fill).astype(BF16)
 
-        ahead = front(0)
+        ahead = [front(h) for h in range(2)]
         for h in range(8):
-            now = ahead
-            if h < 7:
-                ahead = front(h + 1)
+            now = ahead.pop(0)
+            if h + 2 < 8:
+                ahead.append(front(h + 2))
             back(h, now)
         store(slot, at).start()
         return 0
@@ -547,11 +550,11 @@
             put(pairs + pair, (first[1] + dk) * 0.125)
             put(2 * pairs + pair, first[2] + dv)
 
-    ahead = front(0)
+    ahead = [front(0), front(1)]
     for h in range(2 * pairs):
-        now = ahead
-        if h + 1 < 2 * pairs:
-            ahead = front(h + 1)
+        now = ahead.pop(0)
+        if h + 2 < 2 * pairs:
+            ahead.append(front(h + 2))
         back(h, *now)
 
 
@@ -1088,17 +1091,17 @@
     pieces = summed.reshape(48, PIECE, 128)
 
     def qkv_piece(n):
-        def place(i, k):
+        def place(i):
             block = 3 * i + n
             kind, pair = block // 4, block % 4
-            return (36 + 6 * (pair // 2) + 2 * kind + pair % 2, k, 0)
-
-        return pl.BlockSpec((1, PIECE // 2, 128), place)
+            return (36 + 6 * (pair // 2) + 2 * kind + pair % 2, 0, 0)
+
+        return pl.BlockSpec((1, PIECE, 128), place)
 
     shape = jax.ShapeDtypeStruct
     return pl.pallas_call(
         unpack_kernel,
-        grid=(4, 2),
+        grid=(4,),
         out_shape=(
             shape((width, wide), F32),
             shape((width, width), F32),
@@ -1106,16 +1109,16 @@
             shape((hidden, width), F32),
         ),
         in_specs=[
-            pl.BlockSpec((4, PIECE // 2, 128), lambda i, k: (i, k, 0)),
-            pl.BlockSpec((4, PIECE // 2, 128), lambda i, k: (4 + i, k, 0)),
-            pl.BlockSpec((1, PIECE // 2, 128), lambda i, k: (32 + i, k, 0)),
+            pl.BlockSpec((4, PIECE, 128), lambda i: (i, 0, 0)),
+            pl.BlockSpec((4, PIECE, 128), lambda i: (4 + i, 0, 0)),
+            pl.BlockSpec((1, PIECE, 128), lambda i: (32 + i, 0, 0)),
         ]
         + [qkv_piece(n) for n in range(3)],
         out_specs=(
-            pl.BlockSpec((width // 2, wide // 4), lambda i, k: (k, i)),
-            pl.BlockSpec((width // 2, width // 4), lambda i, k: (k, i)),
-            pl.BlockSpec((width // 2, hidden // 4), lambda i, k: (k, i)),
-            pl.BlockSpec((hidden // 8, width), lambda i, k: (2 * i + k, 0)),
+            pl.BlockSpec((width, wide // 4), lambda i: (0, i)),
+            pl.BlockSpec((width, width // 4), lambda i: (0, i)),
+            pl.BlockSpec((width, hidden // 4), lambda i: (0, i)),
+            pl.BlockSpec((hidden // 4, width), lambda i: (i, 0)),
         ),
         compiler_params=pltpu.CompilerParams(vmem_limit_bytes=60 * MIB),
         name="unpack",

time: 205 us -> 194 us (0.946)
  Pallas kernels: 202 us -> 190 us
    pallas_call x1, Pallas kernels: 117 us -> 106 us  [backward(): pl.pallas_call(functools.partial(backward_kernel, devices, (most, local_l...]
where the time goes in v3:
time: 194 us; the launch traced here: 193 us
  Pallas kernels  190 us (98%)
    pallas_call x1, Pallas kernels, backward(): pl.pallas_call(functools.partial(backward_kernel, devices, (most, local_l...  106 us
    pallas_call x1, Pallas kernels, mlp(): pl.pallas_call(functools.partial(mlp_kernel, (max_tiles(local_len), local...  31.6 us
    pallas_call x1, Pallas kernels, attend_forward(): pl.pallas_call(functools.partial(attend_forward_kernel, (most, local_len,...  24 us
    pallas_call x1, Pallas kernels, project(): pl.pallas_call(functools.partial(project_kernel, devices, count // rows),...  20.2 us
    pallas_call x1, Pallas kernels, unpack(): pl.pallas_call(unpack_kernel, grid=(4,), out_shape=(shape((width, wide),...  7.99 us

profile of v3, /device:TPU:0, one launch (start us, length us, event | category | flops | bytes accessed | tf_op | source)
XLA Modules:
  0.0 192.5 jit_solution(973753290155093416)
XLA Ops:
  0.6 20.2 %project.1 = (bf16[2048,1536]{1,0:T(8,128)(2,1)}, bf16[512,2048]{1,0:T(8,128)(2,1)}, bf16[2,2,256,512]{3,2,1,0:T(8,128)(2,1)}) custom-call(bf16[2048,512]{1,0:T(8,128)(2,1)} %bitcast.17, bf16[512,1536]{1,0:T(8,128)(2,1)} %w_qkv.5, f32[1,512]{1,0:T(1,128)} %bitcast.23, bf16[2048,512]{1,0:T(8,128)(2,1)} %bitcast.18), custom_call_target="tpu_custom_call" | custom-call | tf_op jit(solution)/shard_map/project/pallas_call | solution.py:213
  20.9 24.0 %attend_forward.1 = (bf16[2048,512]{1,0:T(8,128)(2,1)}, bf16[18,2,9,256,128]{4,3,2,1,0:T(8,128)(2,1)}, s32[288]{0:T(512)}) custom-call(s32[2,65]{1,0:T(2,128)} %lengths.1, bf16[2048,1536]{1,0:T(8,128)(2,1)} %get-tuple-element.31.local, bf16[2,2,256,512]{3,2,1,0:T(8,128)(2,1)} %get-tuple-element.32.left.right, ...), custom_call_target="tpu_custom_call" | custom-call | tf_op jit(solution)/shard_map/attend_forward/pallas_call | solution.py:347
  44.9 31.6 %mlp.1 = (bf16[2048,512]{1,0:T(8,128)(2,1)}, bf16[8,2048,256]{2,1,0:T(8,128)(2,1)}, bf16[8,2048,256]{2,1,0:T(8,128)(2,1)}, f32[2048,512]{1,0:T(8,128)}, bf16[2,2...) custom-call(s32[288]{0:T(512)} %get-tuple-element.33.table, ...), custom_call_target="tpu_custom_call" | custom-call | tf_op jit(solution)/shard_map/mlp/pallas_call | solution.py:471
  76.5 106.1 %backward.1 = (bf16[2048,512]{1,0:T(8,128)(2,1)}, bf16[24576,128]{1,0:T(8,128)(2,1)}, f32[16,512]{1,0:T(8,128)}) custom-call(s32[288]{0:T(512)} %get-tuple-element.33.table, f32[8,512]{1,0:T(8,128)} %get-tuple-element.36.gains, bf16[512,1536]{1,0:T(8,128)(2,1)} %w_qkv.5, f32[1,512]{1,0:T(1,128)} %bitcast.25, ...), custom_call_target="tpu_custom_call" | custom-call | tf_op jit(solution)/shard_map/backward/pallas_call | solution.py:1031
  182.6 0.0 copy-start.1
  182.6 0.0 copy-start
  182.6 8.0 %unpack.1 = (f32[512,1536]{1,0:T(8,128)}, f32[512,512]{1,0:T(8,128)}, f32[512,2048]{1,0:T(8,128)}, f32[2048,512]{1,0:T(8,128)}) custom-call(bf16[48,512,128]{2,1,0:T(8,128)(2,1)} %bitcast.11, bf16[48,512,128]{2,1,0:T(8,128)(2,1)} %bitcast.12, bf16[48,512,128]{2,1,0:T(8,128)(2,1)} %bitcast.13, bf16[48,512,128]{2,1,0:T(8,128)(2,1)} %bitcast.14, ...), custom_call_target="tpu_custom_call" | custom-call | tf_op jit(solution)/shard_map/unpack/pallas_call | solution.py:1102
  190.6 0.0 copy-done.1
  190.6 0.6 fusion
  191.2 0.0 copy-done
  191.2 1.3 copy.18
  (1 shorter events, 0.0 us)
Async XLA Ops:
  182.6 8.0 %copy-start.1 = (f32[16,512]{1,0:T(8,128)S(1)}, f32[16,512]{1,0:T(8,128)}, u32[]{:S(2)}) copy-start(f32[16,512]{1,0:T(8,128)} %get-tuple-element.53) | copy-start | bytes 98308
  182.6 8.6 %copy-start = (bf16[2048,512]{1,0:T(8,128)(2,1)S(1)}, bf16[2048,512]{1,0:T(8,128)(2,1)}, u32[]{:S(2)}) copy-start(bf16[2048,512]{1,0:T(8,128)(2,1)} %get-tuple-element.47) | copy-start | bytes 6291460

commit v4 on v3

--- a/solution.py
+++ b/solution.py
@@ -964,7 +964,7 @@
         back = normalize_back(d_normed * gain_one[...], normed, scale)
         made_tok[part, :] = (resid[part, :] + back).astype(BF16)
         store_tok(i).start()
-        for k in range(1, blocks, 2):
+        for k in range(2, blocks, 3):
 
             @pl.when(i == k)
             def _():

time: 194 us -> 189 us (0.974)
  Pallas kernels: 190 us -> 185 us
    pallas_call x1, Pallas kernels: 106 us -> 103 us  [backward(): pl.pallas_call(functools.partial(backward_kernel, devices, (most, local_l...]
where the time goes in v4:
time: 189 us; the launch traced here: 188 us
  Pallas kernels  185 us (98%)
  local copies, waits for them, and re-layouts  1.92 us (1%)
    pallas_call x1, Pallas kernels, backward(): pl.pallas_call(functools.partial(backward_kernel, devices, (most, local_l...  103 us
    pallas_call x1, Pallas kernels, mlp(): pl.pallas_call(functools.partial(mlp_kernel, (max_tiles(local_len), local...  31.6 us
    pallas_call x1, Pallas kernels, attend_forward(): pl.pallas_call(functools.partial(attend_forward_kernel, (most, local_len,...  23 us
    pallas_call x1, Pallas kernels, project(): pl.pallas_call(functools.partial(project_kernel, devices, count // rows),...  20.2 us
    pallas_call x1, Pallas kernels, unpack(): pl.pallas_call(unpack_kernel, grid=(4,), out_shape=(shape((width, wide),...  7.99 us

profile of v4, /device:TPU:0, one launch (start us, length us, event | category | flops | bytes accessed | tf_op | source)
XLA Modules:
  0.0 187.9 jit_solution(7431875164962156256)
XLA Ops:
  0.6 20.2 %project.1 = (bf16[2048,1536]{1,0:T(8,128)(2,1)}, bf16[512,2048]{1,0:T(8,128)(2,1)}, bf16[2,2,256,512]{3,2,1,0:T(8,128)(2,1)}) custom-call(bf16[2048,512]{1,0:T(8,128)(2,1)} %bitcast.17, bf16[512,1536]{1,0:T(8,128)(2,1)} %w_qkv.5, f32[1,512]{1,0:T(1,128)} %bitcast.23, bf16[2048,512]{1,0:T(8,128)(2,1)} %bitcast.18), custom_call_target="tpu_custom_call" | custom-call | tf_op jit(solution)/shard_map/project/pallas_call | solution.py:213
  20.9 23.0 %attend_forward.1 = (bf16[2048,512]{1,0:T(8,128)(2,1)}, bf16[18,2,9,256,128]{4,3,2,1,0:T(8,128)(2,1)}, s32[288]{0:T(512)}) custom-call(s32[2,65]{1,0:T(2,128)} %lengths.1, bf16[2048,1536]{1,0:T(8,128)(2,1)} %get-tuple-element.31.local, bf16[2,2,256,512]{3,2,1,0:T(8,128)(2,1)} %get-tuple-element.32.left.right, ...), custom_call_target="tpu_custom_call" | custom-call | tf_op jit(solution)/shard_map/attend_forward/pallas_call | solution.py:347
  43.9 31.6 %mlp.1 = (bf16[2048,512]{1,0:T(8,128)(2,1)}, bf16[8,2048,256]{2,1,0:T(8,128)(2,1)}, bf16[8,2048,256]{2,1,0:T(8,128)(2,1)}, f32[2048,512]{1,0:T(8,128)}, bf16[2,2...) custom-call(s32[288]{0:T(512)} %get-tuple-element.33.table, ...), custom_call_target="tpu_custom_call" | custom-call | tf_op jit(solution)/shard_map/mlp/pallas_call | solution.py:471
  75.4 102.5 %backward.1 = (bf16[2048,512]{1,0:T(8,128)(2,1)}, bf16[24576,128]{1,0:T(8,128)(2,1)}, f32[16,512]{1,0:T(8,128)}) custom-call(s32[288]{0:T(512)} %get-tuple-element.33.table, f32[8,512]{1,0:T(8,128)} %get-tuple-element.36.gains, bf16[512,1536]{1,0:T(8,128)(2,1)} %w_qkv.5, f32[1,512]{1,0:T(1,128)} %bitcast.25, ...), custom_call_target="tpu_custom_call" | custom-call | tf_op jit(solution)/shard_map/backward/pallas_call | solution.py:1031
  178.0 0.0 copy-start.1
  178.0 0.0 copy-start
  178.0 8.0 %unpack.1 = (f32[512,1536]{1,0:T(8,128)}, f32[512,512]{1,0:T(8,128)}, f32[512,2048]{1,0:T(8,128)}, f32[2048,512]{1,0:T(8,128)}) custom-call(bf16[48,512,128]{2,1,0:T(8,128)(2,1)} %bitcast.11, bf16[48,512,128]{2,1,0:T(8,128)(2,1)} %bitcast.12, bf16[48,512,128]{2,1,0:T(8,128)(2,1)} %bitcast.13, bf16[48,512,128]{2,1,0:T(8,128)(2,1)} %bitcast.14, ...), custom_call_target="tpu_custom_call" | custom-call | tf_op jit(solution)/shard_map/unpack/pallas_call | solution.py:1102
  186.0 0.0 copy-done.1
  186.0 0.6 fusion
  186.6 0.0 copy-done
  186.6 1.3 copy.18
  (1 shorter events, 0.0 us)
Async XLA Ops:
  178.0 8.0 %copy-start.1 = (f32[16,512]{1,0:T(8,128)S(1)}, f32[16,512]{1,0:T(8,128)}, u32[]{:S(2)}) copy-start(f32[16,512]{1,0:T(8,128)} %get-tuple-element.53) | copy-start | bytes 98308
  178.0 8.6 %copy-start = (bf16[2048,512]{1,0:T(8,128)(2,1)S(1)}, bf16[2048,512]{1,0:T(8,128)(2,1)}, u32[]{:S(2)}) copy-start(bf16[2048,512]{1,0:T(8,128)(2,1)} %get-tuple-element.47) | copy-start | bytes 6291460

commit v5 on v4

--- a/solution.py
+++ b/solution.py
@@ -19,7 +19,7 @@
 PIECE = 512
 WINDOW = 64
 GROUPS = 2
-MOVES = (6, 13, 20, 27, 34)
+MOVES = (2, 8, 14, 20, 27, 34)
 LATE = 2
 APART = 1
 AHEAD = 5
@@ -841,7 +841,7 @@
             load_b(normed_one_t, 3).start()
             load_tok.start()
             load_resid.start()
-        if n > 0:
+        if 0 < n < 4:
             sums.advance(finish)
         if n < 4:
             ready(8 * (n + 1))

time: 189 us -> 185 us (0.979)
  Pallas kernels: 185 us -> 182 us
    pallas_call x1, Pallas kernels: 103 us -> 98.3 us  [backward(): pl.pallas_call(functools.partial(backward_kernel, devices, (most, local_l...]
where the time goes in v5:
time: 185 us
  Pallas kernels  182 us (98%)
  local copies, waits for them, and re-layouts  1.92 us (1%)
    pallas_call x1, Pallas kernels, backward(): pl.pallas_call(functools.partial(backward_kernel, devices, (most, local_l...  98.3 us
    pallas_call x1, Pallas kernels, mlp(): pl.pallas_call(functools.partial(mlp_kernel, (max_tiles(local_len), local...  31.6 us
    pallas_call x1, Pallas kernels, attend_forward(): pl.pallas_call(functools.partial(attend_forward_kernel, (most, local_len,...  24.1 us
    pallas_call x1, Pallas kernels, project(): pl.pallas_call(functools.partial(project_kernel, devices, count // rows),...  20.2 us
    pallas_call x1, Pallas kernels, unpack(): pl.pallas_call(unpack_kernel, grid=(4,), out_shape=(shape((width, wide),...  7.99 us

profile of v5, /device:TPU:0, one launch (start us, length us, event | category | flops | bytes accessed | tf_op | source)
XLA Modules:
  0.0 184.8 jit_solution(8586748685136242841)
XLA Ops:
  0.6 20.2 %project.1 = (bf16[2048,1536]{1,0:T(8,128)(2,1)}, bf16[512,2048]{1,0:T(8,128)(2,1)}, bf16[2,2,256,512]{3,2,1,0:T(8,128)(2,1)}) custom-call(bf16[2048,512]{1,0:T(8,128)(2,1)} %bitcast.17, bf16[512,1536]{1,0:T(8,128)(2,1)} %w_qkv.5, f32[1,512]{1,0:T(1,128)} %bitcast.23, bf16[2048,512]{1,0:T(8,128)(2,1)} %bitcast.18), custom_call_target="tpu_custom_call" | custom-call | tf_op jit(solution)/shard_map/project/pallas_call | solution.py:213
  20.9 24.1 %attend_forward.1 = (bf16[2048,512]{1,0:T(8,128)(2,1)}, bf16[18,2,9,256,128]{4,3,2,1,0:T(8,128)(2,1)}, s32[288]{0:T(512)}) custom-call(s32[2,65]{1,0:T(2,128)} %lengths.1, bf16[2048,1536]{1,0:T(8,128)(2,1)} %get-tuple-element.31.local, bf16[2,2,256,512]{3,2,1,0:T(8,128)(2,1)} %get-tuple-element.32.left.right, ...), custom_call_target="tpu_custom_call" | custom-call | tf_op jit(solution)/shard_map/attend_forward/pallas_call | solution.py:347
  44.9 31.6 %mlp.1 = (bf16[2048,512]{1,0:T(8,128)(2,1)}, bf16[8,2048,256]{2,1,0:T(8,128)(2,1)}, bf16[8,2048,256]{2,1,0:T(8,128)(2,1)}, f32[2048,512]{1,0:T(8,128)}, bf16[2,2...) custom-call(s32[288]{0:T(512)} %get-tuple-element.33.table, ...), custom_call_target="tpu_custom_call" | custom-call | tf_op jit(solution)/shard_map/mlp/pallas_call | solution.py:471
  76.5 98.3 %backward.1 = (bf16[2048,512]{1,0:T(8,128)(2,1)}, bf16[24576,128]{1,0:T(8,128)(2,1)}, f32[16,512]{1,0:T(8,128)}) custom-call(s32[288]{0:T(512)} %get-tuple-element.33.table, f32[8,512]{1,0:T(8,128)} %get-tuple-element.36.gains, bf16[512,1536]{1,0:T(8,128)(2,1)} %w_qkv.5, f32[1,512]{1,0:T(1,128)} %bitcast.25, ...), custom_call_target="tpu_custom_call" | custom-call | tf_op jit(solution)/shard_map/backward/pallas_call | solution.py:1031
  174.8 0.0 copy-start.1
  174.9 0.0 copy-start
  174.9 8.0 %unpack.1 = (f32[512,1536]{1,0:T(8,128)}, f32[512,512]{1,0:T(8,128)}, f32[512,2048]{1,0:T(8,128)}, f32[2048,512]{1,0:T(8,128)}) custom-call(bf16[48,512,128]{2,1,0:T(8,128)(2,1)} %bitcast.11, bf16[48,512,128]{2,1,0:T(8,128)(2,1)} %bitcast.12, bf16[48,512,128]{2,1,0:T(8,128)(2,1)} %bitcast.13, bf16[48,512,128]{2,1,0:T(8,128)(2,1)} %bitcast.14, ...), custom_call_target="tpu_custom_call" | custom-call | tf_op jit(solution)/shard_map/unpack/pallas_call | solution.py:1102
  182.9 0.0 copy-done.1
  182.9 0.6 fusion
  183.5 0.0 copy-done
  183.5 1.3 copy.18
  (1 shorter events, 0.0 us)
Async XLA Ops:
  174.8 8.0 %copy-start.1 = (f32[16,512]{1,0:T(8,128)S(1)}, f32[16,512]{1,0:T(8,128)}, u32[]{:S(2)}) copy-start(f32[16,512]{1,0:T(8,128)} %get-tuple-element.53) | copy-start | bytes 98308
  174.9 8.6 %copy-start = (bf16[2048,512]{1,0:T(8,128)(2,1)S(1)}, bf16[2048,512]{1,0:T(8,128)(2,1)}, u32[]{:S(2)}) copy-start(bf16[2048,512]{1,0:T(8,128)(2,1)} %get-tuple-element.47) | copy-start | bytes 6291460
